TPU v7x, 128 devices: a whole 4x4x4 slice. The times are simulated.
128 devices in a mesh: fsdp: 32 (over z_lo, y, x), dp: 4 (over z_hi, core).
Axes of the slice: x: 4, y: 4, z: 4 (z_hi: 2, z_lo: 2; z = z_hi * 2 + z_lo), core: 2. Of those that a mesh axis runs over, the one named last changes fastest.
Arguments:
- tokens: bfloat16 [32768, 16384], P(('fsdp', 'dp')), may hold values from -0.75 to 0.75
- key_grads: bfloat16 [32768, 512], P(('fsdp', 'dp')), may hold values from -1 to 1
- old_param: bfloat16 [32768, 512], P('fsdp'), may hold values from -1.5 to 1.5
- old_first: float32 [32768, 512], P('fsdp'), may hold values from -6 to 6
- old_second: float32 [32768, 512], P('fsdp'), may hold values from 0.25 to 4
- old_home: int32 [1024], replicated, may hold values from 0 to 2047, as said below
Outputs:
- keys: bfloat16 [32768, 512], P(('fsdp', 'dp'))
- input_grads: bfloat16 [32768, 16384], P(('fsdp', 'dp'))
- new_param: bfloat16 [16384, 512], P('fsdp')
- new_first: float32 [16384, 512], P('fsdp')
- new_second: float32 [16384, 512], P('fsdp')
Inputs may be any that keep to these rules, and one draw needn't show every extreme that they name: Values are distinct. Each fsdp index holds at most 64 blocks in the old layout, and some index holds exactly 64; at most 2 blocks go from one old owner to one new owner (block b's new owner is b // (1024 // 32), its old owner old_home[b] // 64), and some pair carries exactly 2.
All inputs are finite; a program needn't handle non-finite values.
Results may differ from a plain program's by a relative error of at most 0.004.
Values may be sent and summed in bfloat16 or wider, within the bound.
No kernel may reach another device: no remote copies, remote signals or barrier semaphores. Data moves between devices by JAX's collectives and lax.ppermute only.
A program may use at most 192 MiB of HBM per device.

v0:
```python
import jax
import jax.numpy as jnp
from jax import lax
from jax.sharding import PartitionSpec as P

BR = 16


beta_first = 0.9
beta_second = 0.95
eps_adam = 1e-08
learn_rate = 0.001
decay_rate = 0.1
bias_first = 1.0 - 0.9**10
bias_second = 1.0 - 0.95**10


def pack_blocks(buffer, table, count_dev):
    width = buffer.shape[1]
    blocks = buffer.reshape(-1, BR, width)
    padded = jnp.concatenate([blocks, jnp.zeros((1, BR, width), buffer.dtype)], axis=0)
    chosen = jnp.take(padded, table, axis=0)
    return chosen.reshape(count_dev, -1, width)


def unpack_blocks(received, rows_taken):
    width = received.shape[2]
    blocks = received.reshape(-1, BR, width)
    return jnp.take(blocks, rows_taken, axis=0).reshape(-1, width)


def adamw(weight, first, second, gradient):
    new_first = beta_first * first + (1.0 - beta_first) * gradient
    new_second = beta_second * second + (1.0 - beta_second) * gradient * gradient
    weight_wide = weight.astype(jnp.float32)
    update = (
        new_first / bias_first / (jnp.sqrt(new_second / bias_second) + eps_adam)
        + decay_rate * weight_wide
    )
    return ((weight_wide - learn_rate * update).astype(jnp.bfloat16), new_first, new_second)


def on_device(tokens, key_grads, old_param, old_first, old_second, old_home):
    count_dev = lax.axis_size("fsdp")
    my_index = lax.axis_index("fsdp")
    slots = old_param.shape[0] // BR
    blocks_all = old_home.shape[0]
    per_dest = blocks_all // count_dev
    pair = 2 * per_dest // count_dev
    source = old_home // slots
    source_grid = source.reshape(count_dev, per_dest)
    idx = jnp.arange(per_dest)
    earlier = idx[None, :, None] > idx[None, None, :]
    same_source = source_grid[:, :, None] == source_grid[:, None, :]
    pair_rank = jnp.sum((same_source & earlier).astype(jnp.int32), axis=2)
    position = (jnp.arange(count_dev, dtype=jnp.int32)[:, None] * pair + pair_rank).reshape(
        blocks_all
    )
    target = jnp.where(source == my_index, position, count_dev * pair)
    table = (
        jnp.full((count_dev * pair,), slots, jnp.int32)
        .at[target]
        .set(old_home % slots, mode="drop")
    )
    my_source = lax.dynamic_slice_in_dim(source, my_index * per_dest, per_dest)
    my_rank = lax.dynamic_index_in_dim(pair_rank, my_index, 0, keepdims=False)
    rows_taken = my_source * pair + my_rank
    sent_param = pack_blocks(old_param, table, count_dev)
    got_param = lax.all_to_all(sent_param, "fsdp", split_axis=0, concat_axis=0, tiled=True)
    weight = unpack_blocks(got_param, rows_taken)
    sent_first = pack_blocks(old_first, table, count_dev)
    sent_second = pack_blocks(old_second, table, count_dev)
    got_first, got_second = (
        lax.all_to_all(sent_first, "fsdp", split_axis=0, concat_axis=0, tiled=True),
        lax.all_to_all(sent_second, "fsdp", split_axis=0, concat_axis=0, tiled=True),
    )
    first = unpack_blocks(got_first, rows_taken)
    second = unpack_blocks(got_second, rows_taken)
    piece = lax.all_gather(weight, "fsdp", axis=0, tiled=True)
    columns = tokens
    key_total = jnp.dot(columns, piece, preferred_element_type=jnp.float32)
    back = lax.dot_general(
        key_grads, piece, (((1,), (1,)), ((), ())), preferred_element_type=jnp.float32
    )
    grads_in = back.astype(jnp.bfloat16)
    key_total, input_grads = (key_total, grads_in)
    keys = key_total.astype(jnp.bfloat16)
    partial_grad = None
    columns = tokens
    partial_grad = lax.psum_scatter(
        lax.dot_general(
            columns, key_grads, (((0,), (0,)), ((), ())), preferred_element_type=jnp.float32
        ).astype(jnp.bfloat16),
        "fsdp",
        scatter_dimension=0,
        tiled=True,
    ).astype(jnp.float32)
    gradient = lax.psum(partial_grad, "dp")
    new_param, new_first, new_second = adamw(weight, first, second, gradient)
    return (keys, input_grads, new_param, new_first, new_second)


def solution(mesh):
    in_specs = (
        P(("fsdp", "dp"), None),
        P(("fsdp", "dp"), None),
        P("fsdp", None),
        P("fsdp", None),
        P("fsdp", None),
        P(),
    )
    out_specs = (
        P(("fsdp", "dp"), None),
        P(("fsdp", "dp"), None),
        P("fsdp", None),
        P("fsdp", None),
        P("fsdp", None),
    )
    return jax.shard_map(
        on_device, mesh=mesh, in_specs=in_specs, out_specs=out_specs, check_vma=False
    )
```

profile of v0, /device:TPU:1, one launch (start us, length us, event | category | flops | bytes accessed | tf_op | source)
XLA Modules:
  0.0 547.8 jit_solution(11229948568046897958)
XLA Ops:
  7.2 0.9 copy-done
  8.1 11.7 %convolution_convert_fusion = bf16[16384,512]{1,0:T(8,128)(2,1)} fusion(bf16[256,16384]{1,0:T(8,128)(2,1)} %param.10, bf16[256,512]{1,0:T(8,128)(2,1)S(1)} %copy-done), kind=kOutput, calls=%fused_computation.7 | convolution fusion | flops 4303355904 | bytes 25427968 | tf_op jit(solution)/shard_map/dot_general | solution.py:91
  19.8 0.7 copy-done.3
  20.6 0.8 convert_reduce_fusion
  21.5 4.3 scatter_custom_fusion
  25.8 0.1 broadcast_in_dim.69
  26.0 0.1 copy.17
  26.3 0.6 gather_fusion
  26.9 1.2 bitcast_select_fusion
  28.1 9.2 %all-to-all-start = ((bf16[32,32,512]{2,1,0:T(8,128)(2,1)}), bf16[32,32,512]{2,1,0:T(8,128)(2,1)S(1)}, u32[]{:S(2)}, u32[]{:S(2)}) async-start(bf16[32,32,512]{2,1,0:T(8,128)(2,1)} %bitcast_select_fusion), calls=%async_computation | async-start | bytes 2097152 | tf_op jit(solution)/shard_map/all_to_all | solution.py:69
  37.3 1.8 concatenate.10
  39.1 2.0 gather_fusion.2
  41.1 1.8 concatenate.11
  42.9 2.0 gather_fusion.4
  44.9 3.9 broadcast_select_fusion
  48.9 30.5 %all-to-all-done = bf16[32,32,512]{2,1,0:T(8,128)(2,1)S(1)} async-done(((bf16[32,32,512]{2,1,0:T(8,128)(2,1)}), bf16[32,32,512]{2,1,0:T(8,128)(2,1)S(1)}, u32[]{:S(2)}, u32[]{:S(2)}) %all-to-all-start) | async-done | bytes 1048608 | tf_op jit(solution)/shard_map/all_to_all | solution.py:69
  79.3 62.5 %all_to_all.15 = f32[32,32,512]{2,1,0:T(8,128)} all-to-all(f32[32,32,512]{2,1,0:T(8,128)S(1)} %bitcast.37), channel_id=1, replica_groups=mesh['fsdp'=32,'dp'=4] {'fsdp'}, dimensions={0} | all-to-all | bytes 4194304 | tf_op jit(solution)/shard_map/all_to_all | solution.py:74
  141.8 8.1 %all-to-all-start.2 = ((f32[32,32,512]{2,1,0:T(8,128)}), f32[32,32,512]{2,1,0:T(8,128)S(1)}, u32[]{:S(2)}, u32[]{:S(2)}) async-start(f32[32,32,512]{2,1,0:T(8,128)} %bitcast.13), calls=%async_computation.3 | async-start | bytes 4194304 | tf_op jit(solution)/shard_map/all_to_all | solution.py:75
  150.1 0.1 broadcast_in_dim.65
  150.2 1.4 gather_fusion.1
  151.6 2.2 gather_fusion.3
  153.8 41.0 %all-to-all-done.2 = f32[32,32,512]{2,1,0:T(8,128)S(1)} async-done(((f32[32,32,512]{2,1,0:T(8,128)}), f32[32,32,512]{2,1,0:T(8,128)S(1)}, u32[]{:S(2)}, u32[]{:S(2)}) %all-to-all-start.2) | async-done | bytes 2097184 | tf_op jit(solution)/shard_map/all_to_all | solution.py:75
  194.9 1.6 gather_fusion.5
  196.5 1.5 select_multiply_fusion
  198.0 72.5 %reduce-scatter.2.cloned.1.call-done = bf16[512,512]{1,0:T(8,128)(2,1)} async-done(((bf16[16384,512]{1,0:T(8,128)(2,1)}), bf16[512,512]{1,0:T(8,128)(2,1)}) %reduce-scatter.2.cloned.1.call-update) | async-done | bytes 524304 | tf_op jit(solution)/shard_map/reduce_scatter | solution.py:90
  270.5 44.1 %all-reduce.4 = f32[512,512]{1,0:T(8,128)S(1)} all-reduce(bf16[512,512]{1,0:T(8,128)(2,1)} %reduce-scatter.2.cloned.1.call-done), channel_id=1, replica_groups=mesh['fsdp'=32,'dp'=4] {'dp'}, use_global_device_ids=true, to_apply=%region_3.6 | all-reduce | flops 262144 | bytes 1572864 | tf_op jit(solution)/shard_map/psum | solution.py:98
  314.6 3.7 fusion.4
  318.3 183.6 %all-gather.2.cloned.1.call-done = bf16[16384,512]{1,0:T(8,128)(2,1)} async-done(((bf16[512,512]{1,0:T(8,128)(2,1)}), bf16[16384,512]{1,0:T(8,128)(2,1)}) %all-gather.2.cloned.1.call-update) | async-done | bytes 16777232 | tf_op jit(solution)/shard_map/all_gather | solution.py:79
  501.9 13.6 %fusion = bf16[256,16384]{0,1:T(8,128)(2,1)} fusion(bf16[16384,512]{1,0:T(8,128)(2,1)} %all-gather.2.cloned.1.call-done, bf16[256,512]{1,0:T(8,128)(2,1)S(1)} %copy-done), kind=kOutput, calls=%fused_computation.9 | convolution fusion | flops 4299161600 | bytes 25427968 | tf_op jit(solution)/shard_map/dot_general | solution.py:82
  515.5 11.9 %copy.20 = bf16[256,16384]{1,0:T(8,128)(2,1)} copy(bf16[256,16384]{0,1:T(8,128)(2,1)} %fusion) | data formatting | bytes 16777216
  527.4 12.7 %fusion.1 = bf16[256,512]{0,1:T(8,128)(2,1)S(1)} fusion(bf16[16384,512]{1,0:T(8,128)(2,1)} %all-gather.2.cloned.1.call-done, bf16[256,16384]{1,0:T(8,128)(2,1)} %param.10), kind=kOutput, calls=%fused_computation.14 | convolution fusion | flops 4295098368 | bytes 25427968 | tf_op jit(solution)/shard_map/dot_general | solution.py:81
  540.1 0.8 copy.19
  (26 shorter events, 0.7 us)
Async XLA Ops:
  7.2 1.0 copy-start
  7.2 263.3 %reduce-scatter.2.cloned.1.call-start = ((), (), s32[]{:S(2)}) async-start(), calls=%async_computation.5 | async-start | bytes 17301504 | tf_op jit(solution)/shard_map/reduce_scatter | solution.py:90
  19.8 0.7 copy-start.3
  19.8 6.4 %copy-start.2 = (bf16[1024,512]{1,0:T(8,128)(2,1)S(1)}, bf16[1024,512]{1,0:T(8,128)(2,1)}, u32[]{:S(2)}) copy-start(bf16[1024,512]{1,0:T(8,128)(2,1)} %param.12) | copy-start | bytes 3145732
  28.1 51.3 %all-to-all-start = ((bf16[32,32,512]{2,1,0:T(8,128)(2,1)}), bf16[32,32,512]{2,1,0:T(8,128)(2,1)S(1)}, u32[]{:S(2)}, u32[]{:S(2)}) async-start(bf16[32,32,512]{2,1,0:T(8,128)(2,1)} %bitcast_select_fusion), calls=%async_computation | async-start | bytes 2097152 | tf_op jit(solution)/shard_map/all_to_all | solution.py:69
  141.8 53.1 %all-to-all-start.2 = ((f32[32,32,512]{2,1,0:T(8,128)}), f32[32,32,512]{2,1,0:T(8,128)S(1)}, u32[]{:S(2)}, u32[]{:S(2)}) async-start(f32[32,32,512]{2,1,0:T(8,128)} %bitcast.13), calls=%async_computation.3 | async-start | bytes 4194304 | tf_op jit(solution)/shard_map/all_to_all | solution.py:75
  149.9 352.0 %all-gather.2.cloned.1.call-start = ((), (), s32[]{:S(2)}) async-start(), calls=%async_computation.4 | async-start | bytes 17301504 | tf_op jit(solution)/shard_map/all_gather | solution.py:79
  527.4 13.6 %copy-start.1 = (bf16[256,512]{1,0:T(8,128)(2,1)S(1)}, bf16[256,512]{1,0:T(8,128)(2,1)}, u32[]{:S(2)}) copy-start(bf16[256,512]{1,0:T(8,128)(2,1)} %param.11) | copy-start | bytes 786436
Sparse Core Ops, SparseCore 0:
  19.9 250.4 reduce-scatter.1
  318.4 183.4 all-gather.1
where the time goes:
time: 554 us; the launch traced here: 548 us
  waiting for transfers between devices  328 us (59%)
  blocking collectives  107 us (19%)
  matrix products  37.9 us (7%)
  local copies, waits for them, and re-layouts  32.7 us (6%)
  starting transfers between devices  17.4 us (3%)
  between operations  14.2 us (3%)
  other arithmetic  11.3 us (2%)
    all_gather x1, waiting for transfers between devices, on_device(): piece = lax.all_gather(weight, 'fsdp', axis=0, tiled=True)  184 us
    reduce_scatter x1, waiting for transfers between devices, on_device(): lax.psum_scatter(lax.dot_general(columns, key_grads, (((0,), (0,)), ((),...  72.5 us
    all_to_all x1, blocking collectives, on_device(): lax.all_to_all(sent_first, 'fsdp', split_axis=0, concat_axis=0, tiled=True)  62.5 us
    psum x1, blocking collectives, on_device(): gradient = lax.psum(partial_grad, 'dp')  44.1 us
    all_to_all x1, waiting for transfers between devices, on_device(): lax.all_to_all(sent_second, 'fsdp', split_axis=0, concat_axis=0, tiled=True)  41 us
    all_to_all x1, waiting for transfers between devices, on_device(): lax.all_to_all(sent_param, 'fsdp', split_axis=0, concat_axis=0, tiled=True)  30.5 us
    unnamed x10, local copies, waits for them, and re-layouts  14.3 us
    dot_general x1, matrix products, on_device(): lax.dot_general(key_grads, piece, (((1,), (1,)), ((), ())), preferred_ele...  13.6 us
  transfers between devices with their start and end apart: 4, of which 4 were waited for; matrix products, arithmetic and copies ran while one was open for 5% of the time, Pallas kernels for 0%

commit v1 on v0

v1 whole, which is shorter than its diff:
```python
import functools
import itertools

import jax
import jax.numpy as jnp
from jax import lax
from jax.experimental import pallas as pl
from jax.experimental.pallas import tpu as pltpu
from jax.sharding import PartitionSpec as P

BR = 16
C = 512
HALF = 256
QUARTER = 128
BIG = 352
SMALL = C - BIG
TOK = 256
D = 16384
NF = 32

beta_first = 0.9
beta_second = 0.95
eps_adam = 1e-08
learn_rate = 0.001
decay_rate = 0.1
bias_first = 1.0 - 0.9**10
bias_second = 1.0 - 0.95**10

AXES = ("fsdp", "dp")
bf16 = jnp.bfloat16
f32 = jnp.float32
ANY = pl.BlockSpec(memory_space=pl.ANY)
SMEM = pl.BlockSpec(memory_space=pltpu.SMEM)
VMEM = pl.BlockSpec(memory_space=pltpu.VMEM)


def device_number(x, y, zl, zh, core):
    return (((zl * 4 + y) * 4 + x) * 2 + zh) * 2 + core


def shift_pairs(axis_of_core, shift):
    pairs = []
    for x, y, zl, zh, core in itertools.product(range(4), range(4), range(2), range(2), range(2)):
        to = {"x": x, "y": y, "l": zl, "h": zh, "c": core}
        axis = axis_of_core[core]
        to[axis] = (to[axis] + shift) % (4 if axis in "xy" else 2)
        pairs.append(
            (
                device_number(x, y, zl, zh, core),
                device_number(to["x"], to["y"], to["l"], to["h"], to["c"]),
            )
        )
    return pairs


def send(array, axis_of_core, shift=1):
    return lax.ppermute(array, AXES, shift_pairs(axis_of_core, shift))


OUTER = "xy"
INNER = "yx"
PAIR = "ll"
REPLICA = "hh"
CORE = "cc"


def split_kernel(place, tokens, key_grads, out, sem):
    core = place[3]
    copies = []
    for i in range(NF):
        at = pl.multiple_of(i * C + (1 - core) * HALF, HALF)
        copies.append(
            pltpu.make_async_copy(
                tokens.at[:, pl.ds(at, HALF)], out.at[:, pl.ds(i * HALF, HALF)], sem.at[i]
            )
        )
    copies.append(pltpu.make_async_copy(key_grads, out.at[:, pl.ds(D // 2, C)], sem.at[NF]))
    for copy in copies:
        copy.start()
    for copy in copies:
        copy.wait()


def split_tokens(place, tokens, key_grads):
    return pl.pallas_call(
        split_kernel,
        out_shape=jax.ShapeDtypeStruct((TOK, D // 2 + C), bf16),
        in_specs=[SMEM, ANY, ANY],
        out_specs=ANY,
        scratch_shapes=[pltpu.SemaphoreType.DMA((NF + 1,))],
        cost_estimate=pl.CostEstimate(flops=0, bytes_accessed=2**23, transcendentals=0),
    )(place, tokens, key_grads)


def pack_kernel(place, table, param, first, second, out):
    def body(k, carry):
        src = pl.multiple_of(table[k] * BR, BR)
        dst = pl.multiple_of(k * BR, BR)
        out[pl.ds(dst, BR), :HALF] = param[pl.ds(src, BR), :]
        out[pl.ds(dst, BR), HALF : HALF + QUARTER] = first[pl.ds(src, BR), :].astype(bf16)
        out[pl.ds(dst, BR), HALF + QUARTER :] = second[pl.ds(src, BR), :].astype(bf16)
        return carry

    lax.fori_loop(0, 2 * NF, body, 0, unroll=4)


def pack(place, table, param, first, second):
    rows = param.shape[0]
    quarter = lambda i, place, table: (0, place[3] * 2 + place[4])
    return pl.pallas_call(
        pack_kernel,
        out_shape=jax.ShapeDtypeStruct((2 * NF * BR, C), bf16),
        grid_spec=pltpu.PrefetchScalarGridSpec(
            num_scalar_prefetch=2,
            grid=(1,),
            in_specs=[
                pl.BlockSpec((rows, HALF), lambda i, place, table: (0, place[3])),
                pl.BlockSpec((rows, QUARTER), quarter),
                pl.BlockSpec((rows, QUARTER), quarter),
            ],
            out_specs=pl.BlockSpec((2 * NF * BR, C), lambda i, place, table: (0, 0)),
        ),
        compiler_params=pltpu.CompilerParams(vmem_limit_bytes=2**24),
        cost_estimate=pl.CostEstimate(flops=0, bytes_accessed=3 * 2**20, transcendentals=0),
    )(place, table, param, first, second)


def unpack_kernel(rows_taken, got, weight, moments):
    def body(k, carry):
        src = pl.multiple_of(rows_taken[k] * BR, BR)
        dst = pl.multiple_of(k * BR, BR)
        weight[pl.ds(dst, BR), :] = got[pl.ds(src, BR), :HALF]
        moments[pl.ds(dst, BR), :] = got[pl.ds(src, BR), HALF:]
        return carry

    lax.fori_loop(0, NF, body, 0, unroll=4)


def unpack(rows_taken, got):
    half = jax.ShapeDtypeStruct((C, HALF), bf16)
    return pl.pallas_call(
        unpack_kernel,
        out_shape=(half, half),
        in_specs=[SMEM, VMEM],
        out_specs=(VMEM, VMEM),
        compiler_params=pltpu.CompilerParams(vmem_limit_bytes=2**23),
        cost_estimate=pl.CostEstimate(flops=0, bytes_accessed=2 * 2**20, transcendentals=0),
    )(rows_taken, got)


def target_index(place, core, outer, pair, inner, sign):
    x, y, zl = place[0], place[1], place[2]
    along_x = jnp.where(core == 0, outer, inner)
    along_y = jnp.where(core == 0, inner, outer)
    to_x = lax.rem(x + sign * along_x + 4, 4)
    to_y = lax.rem(y + sign * along_y + 4, 4)
    to_z = lax.rem(zl + pair, 2)
    return (to_z * 4 + to_y) * 4 + to_x


def gradient_kernel(place, tokens, theirs, key_grads, *refs):
    big, small = refs[0:4], refs[4:6]
    held, made, other_grads, grads_t, sem_in, sem_grads, sem_big, sem_small = refs[6:]
    core = place[3]
    grads_copy = pltpu.make_async_copy(
        theirs.at[:, pl.ds(D // 2, C)], other_grads, sem_grads
    )
    grads_copy.start()

    def loads(i, f):
        mine = pltpu.make_async_copy(
            tokens.at[:, pl.ds(pl.multiple_of(f * C + core * HALF, HALF), HALF)],
            held.at[i, pl.ds(0, TOK)],
            sem_in.at[0, i],
        )
        other = pltpu.make_async_copy(
            theirs.at[:, pl.ds(pl.multiple_of(f * HALF, HALF), HALF)],
            held.at[i, pl.ds(TOK, TOK)],
            sem_in.at[1, i],
        )
        return mine, other

    def start(i, carry):
        outer, rest = lax.div(i, 8), lax.rem(i, 8)
        f = target_index(place, core, outer, lax.div(rest, 4), lax.rem(rest, 4), 1)
        for copy in loads(i, f):
            copy.start()
        return carry

    lax.fori_loop(0, NF, start, 0)
    grads_t[:, :TOK] = key_grads[...].T
    grads_copy.wait()
    grads_t[:, TOK:] = other_grads[...].T
    for outer in range(4):
        for pair in range(2):

            def body(inner, carry, outer=outer, pair=pair):
                i = outer * 8 + pair * 4 + inner
                for copy in loads(i, 0):
                    copy.wait()
                made[i] = jnp.dot(
                    grads_t[...], held[i], preferred_element_type=f32
                ).astype(bf16)
                pltpu.make_async_copy(
                    made.at[i, pl.ds(0, BIG)], big[outer].at[pair, inner], sem_big.at[outer]
                ).start()
                pltpu.make_async_copy(
                    made.at[i, pl.ds(BIG, SMALL)], small[pair].at[outer, inner], sem_small.at[pair]
                ).start()
                return carry

            lax.fori_loop(0, 4, body, 0)
    for outer in range(4):
        pltpu.make_async_copy(big[outer], big[outer], sem_big.at[outer]).wait()
    for pair in range(2):
        pltpu.make_async_copy(small[pair], small[pair], sem_small.at[pair]).wait()


def gradient_terms(place, tokens, theirs, key_grads):
    big = jax.ShapeDtypeStruct((2, 4, BIG, HALF), bf16)
    small = jax.ShapeDtypeStruct((4, 4, SMALL, HALF), bf16)
    return pl.pallas_call(
        gradient_kernel,
        out_shape=(big,) * 4 + (small,) * 2,
        in_specs=[SMEM, ANY, ANY, VMEM],
        out_specs=(ANY,) * 6,
        scratch_shapes=[
            pltpu.VMEM((NF, 2 * TOK, HALF), bf16),
            pltpu.VMEM((NF, C, HALF), bf16),
            pltpu.VMEM((TOK, C), bf16),
            pltpu.VMEM((C, 2 * TOK), bf16),
            pltpu.SemaphoreType.DMA((2, NF)),
            pltpu.SemaphoreType.DMA,
            pltpu.SemaphoreType.DMA((4,)),
            pltpu.SemaphoreType.DMA((2,)),
        ],
        compiler_params=pltpu.CompilerParams(vmem_limit_bytes=28 * 2**20),
        cost_estimate=pl.CostEstimate(
            flops=2 * 512 * 512 * 8192, bytes_accessed=2**24, transcendentals=0
        ),
    )(place, tokens, theirs, key_grads)


def final_kernel(place, tokens, key_grads, *refs):
    big, small = (refs[0:4], refs[6:10]), (refs[4:6], refs[10:12])
    keys, input_grads = refs[12:14]
    weight, held, made, total, sem_w, sem_in, sem_out = refs[14:]
    core = place[3]

    def at(i):
        sx, rest = lax.div(i, 8), lax.rem(i, 8)
        t, sy = lax.div(rest, 4), lax.rem(rest, 4)
        return sx, t, sy, target_index(place, 0, sx, t, sy, -1)

    def pieces(i, of, outer_big, outer_small, own_core, outer, t, inner):
        col = pl.ds(pl.multiple_of(own_core * HALF, HALF), HALF)
        return (
            lambda: pltpu.make_async_copy(
                big[of][outer_big].at[t, inner],
                weight.at[i, pl.ds(0, BIG), col],
                sem_w.at[2 * of, i],
            ),
            lambda: pltpu.make_async_copy(
                small[of][outer_small].at[outer, inner],
                weight.at[i, pl.ds(BIG, SMALL), col],
                sem_w.at[2 * of + 1, i],
            ),
        )

    def start(i, carry):
        sx, t, sy, f = at(i)
        pltpu.make_async_copy(
            tokens.at[:, pl.ds(pl.multiple_of(f * C, C), C)], held.at[i], sem_in.at[i]
        ).start()
        for of in range(2):
            own_core = core if of == 0 else 1 - core
            outer = jnp.where(own_core == 0, sx, sy)
            inner = jnp.where(own_core == 0, sy, sx)
            for k in range(4):

                @pl.when(outer == k)
                def _(k=k, of=of, own_core=own_core, outer=outer, inner=inner):
                    pieces(i, of, k, 0, own_core, outer, t, inner)[0]().start()

            for k in range(2):

                @pl.when(t == k)
                def _(k=k, of=of, own_core=own_core, outer=outer, inner=inner):
                    pieces(i, of, 0, k, own_core, outer, t, inner)[1]().start()

        return carry

    lax.fori_loop(0, NF, start, 0)
    total[...] = jnp.zeros_like(total)

    def body(i, carry):
        _, _, _, f = at(i)
        pltpu.make_async_copy(tokens.at[:, pl.ds(0, C)], held.at[i], sem_in.at[i]).wait()
        for of in range(2):
            for copy in pieces(i, of, 0, 0, of, 0, 0, 0):
                copy().wait()
        total[...] += jnp.dot(held[i], weight[i], preferred_element_type=f32)
        made[i] = lax.dot_general(
            key_grads[...], weight[i], (((1,), (1,)), ((), ())), preferred_element_type=f32
        ).astype(bf16)
        pltpu.make_async_copy(
            made.at[i], input_grads.at[:, pl.ds(pl.multiple_of(f * C, C), C)], sem_out
        ).start()
        return carry

    lax.fori_loop(0, NF, body, 0)
    keys[...] = total[...].astype(bf16)
    pltpu.make_async_copy(input_grads, input_grads, sem_out).wait()


def final_products(place, tokens, key_grads, pieces):
    return pl.pallas_call(
        final_kernel,
        out_shape=(
            jax.ShapeDtypeStruct((TOK, C), bf16),
            jax.ShapeDtypeStruct((TOK, D), bf16),
        ),
        in_specs=[SMEM, ANY, VMEM] + [ANY] * 12,
        out_specs=(VMEM, ANY),
        scratch_shapes=[
            pltpu.VMEM((NF, C, C), bf16),
            pltpu.VMEM((NF, TOK, C), bf16),
            pltpu.VMEM((NF, TOK, C), bf16),
            pltpu.VMEM((TOK, C), f32),
            pltpu.SemaphoreType.DMA((4, NF)),
            pltpu.SemaphoreType.DMA((NF,)),
            pltpu.SemaphoreType.DMA,
        ],
        compiler_params=pltpu.CompilerParams(vmem_limit_bytes=44 * 2**20),
        cost_estimate=pl.CostEstimate(
            flops=4 * 256 * 512 * 16384, bytes_accessed=2**25, transcendentals=0
        ),
    )(place, tokens, key_grads, *pieces)


def routes(old_home, f, slots):
    home = old_home.reshape(NF, NF)
    source = home // slots
    idx = jnp.arange(NF)
    earlier = idx[None, :, None] > idx[None, None, :]
    same = source[:, :, None] == source[:, None, :]
    rank = jnp.sum((same & earlier).astype(jnp.int32), axis=2)
    mine = source == f
    slot = jnp.where(mine, home % slots, 0)
    table = jnp.stack([jnp.sum(jnp.where(rank == r, slot, 0), axis=1) for r in range(2)], axis=1)
    arrives = source * 2 + rank
    rows_taken = jnp.sum(jnp.where(idx[:, None] == f, arrives, 0), axis=0)
    return table.reshape(2 * NF), rows_taken


def add(*terms):
    total = terms[0].astype(f32)
    for term in terms[1:]:
        total = total + term.astype(f32)
    return total


def reduce_scatter(big, small):
    got_big = [send(big[s], OUTER, s) for s in (2, 1, 3)]
    got_small = send(small[1], PAIR)
    away = add(big[0][1], *[g[1] for g in got_big]).astype(bf16)
    got_away = send(away, PAIR)
    v = [add(small[0][s], got_small[s]).astype(bf16) for s in range(4)]
    got_v = [send(v[s], OUTER, s) for s in (2, 1, 3)]
    u = [
        add(big[0][0, s], *[g[0, s] for g in got_big], got_away[s]).astype(bf16) for s in range(4)
    ]
    w = [add(v[0][s], *[g[s] for g in got_v]).astype(bf16) for s in range(4)]
    whole = [jnp.concatenate([u[s], w[s]], axis=0) for s in range(4)]
    got = [send(whole[s], INNER, s) for s in (2, 1, 3)]
    return add(whole[0], *got)


def all_gather(seed):
    first = [seed] + [send(seed, INNER, s) for s in (1, 2, 3)]
    big = jnp.stack([p[:BIG] for p in first])
    small = jnp.stack([p[BIG:] for p in first])
    big = jnp.stack([big, send(big, PAIR)])
    small = jnp.stack([small] + [send(small, OUTER, s) for s in (1, 2, 3)])
    bigs = {s: send(big, OUTER, s) for s in (2, 1, 3)}
    return (big, bigs[1], bigs[2], bigs[3], small, send(small, PAIR))


def adamw_kernel(place, grads, weights, moments, *refs):
    grads_other, weights_other, moments_other, new_param, new_first, new_second = refs

    def update(core):
        for r in range(2):
            rows = pl.ds(r * HALF, HALF)
            turned = (grads if r == core else grads_other)[...].T
            for c in range(2):
                cols = pl.ds(c * HALF, HALF)
                m = moments if c == core else moments_other
                weight = (weights if c == core else weights_other)[rows, :].astype(f32)
                gradient = turned[:, c * HALF : (c + 1) * HALF]
                first = beta_first * m[rows, :HALF].astype(f32) + (1.0 - beta_first) * gradient
                second = (
                    beta_second * m[rows, HALF:].astype(f32)
                    + (1.0 - beta_second) * gradient * gradient
                )
                step = (
                    first / bias_first / (jnp.sqrt(second / bias_second) + eps_adam)
                    + decay_rate * weight
                )
                new_first[rows, cols] = first
                new_second[rows, cols] = second
                new_param[rows, cols] = (weight - learn_rate * step).astype(bf16)

    for core in range(2):
        pl.when(place[3] == core)(functools.partial(update, core))


def adamw(place, own, other):
    wide = jax.ShapeDtypeStruct((C, C), f32)
    return pl.pallas_call(
        adamw_kernel,
        out_shape=(jax.ShapeDtypeStruct((C, C), bf16), wide, wide),
        in_specs=[SMEM] + [VMEM] * 6,
        out_specs=(VMEM,) * 3,
        compiler_params=pltpu.CompilerParams(vmem_limit_bytes=2**24),
        cost_estimate=pl.CostEstimate(flops=2**22, bytes_accessed=6 * 2**20, transcendentals=2**18),
    )(place, *own, *other)


def ordered(index, own, other, axis):
    low = jnp.where(index == 0, own, other)
    high = jnp.where(index == 0, other, own)
    return jnp.concatenate([low, high], axis=axis)


def on_device(tokens, key_grads, old_param, old_first, old_second, old_home):
    f = lax.axis_index("fsdp").astype(jnp.int32)
    d = lax.axis_index("dp").astype(jnp.int32)
    core, zh = d % 2, d // 2
    place = jnp.stack([f % 4, (f // 4) % 4, f // 16, core, zh])

    theirs = send(split_tokens(place, tokens, key_grads), CORE)
    terms = gradient_terms(place, tokens, theirs, key_grads)

    table, rows_taken = routes(old_home, f, old_param.shape[0] // BR)
    packed = pack(place, table, old_param, old_first, old_second)
    got = lax.all_to_all(packed, "fsdp", split_axis=0, concat_axis=0, tiled=True)
    seed, moments = unpack(rows_taken, got)

    partial = reduce_scatter(terms[:4], terms[4:]).astype(bf16)
    own = all_gather(seed)
    other = tuple(send(p, CORE) for p in own)
    keys, input_grads = final_products(place, tokens, key_grads, own + other)

    moments_zh = send(moments, REPLICA)
    halves = jnp.concatenate(
        [
            ordered(zh, moments[:, :QUARTER], moments_zh[:, :QUARTER], 1),
            ordered(zh, moments[:, QUARTER:], moments_zh[:, QUARTER:], 1),
        ],
        axis=1,
    )
    halves_other = send(halves, CORE)
    seed_other = jnp.concatenate([other[0][0, 0], other[4][0, 0]], axis=0)

    gradient = partial.astype(f32) + send(partial, REPLICA).astype(f32)
    new_param, new_first, new_second = adamw(
        place, (gradient, seed, halves), (send(gradient, CORE), seed_other, halves_other)
    )
    return (keys, input_grads, new_param, new_first, new_second)


def solution(mesh):
    over_all = P(("fsdp", "dp"), None)
    over_fsdp = P("fsdp", None)
    return jax.shard_map(
        on_device,
        mesh=mesh,
        in_specs=(over_all, over_all, over_fsdp, over_fsdp, over_fsdp, P()),
        out_specs=(over_all, over_all, over_fsdp, over_fsdp, over_fsdp),
        check_vma=False,
    )
```

time: 554 us -> 357 us (0.64); the launches traced: 548 us -> 357 us
  waiting for transfers between devices: 328 us -> 65.2 us
  Pallas kernels: 0 us -> 186 us
  blocking collectives: 107 us -> 24.9 us
  starting transfers between devices: 17.4 us -> 64.2 us
  matrix products: 37.9 us -> 0 us
  local copies, waits for them, and re-layouts: 32.7 us -> 6.74 us
  between operations: 14.2 us -> 1.13 us
    pallas_call x0 -> x6, Pallas kernels: none -> 186 us  [the longest x1 137 us: split_tokens(): pl.pallas_call(split_kernel, out_shape=jax.ShapeDtypeStruct((TOK, D // 2...]
    all_gather x1 -> x0, waiting for transfers between devices: 184 us -> none  [on_device(): piece = lax.all_gather(weight, 'fsdp', axis=0, tiled=True)]
    reduce_scatter x1 -> x0, waiting for transfers between devices: 72.5 us -> none  [on_device(): lax.psum_scatter(lax.dot_general(columns, key_grads, (((0,), (0,)), ((),...]
    all_to_all x2 -> x0, waiting for transfers between devices: 71.5 us -> none  [the longest x1 41 us: on_device(): lax.all_to_all(sent_second, 'fsdp', split_axis=0, concat_axis=0, tiled=True)]
    ppermute x0 -> x33, waiting for transfers between devices: none -> 65.2 us  [send(): return lax.ppermute(array, AXES, shift_pairs(axis_of_core, shift))]
    ppermute x0 -> x33, starting transfers between devices: none -> 64.2 us  [send(): return lax.ppermute(array, AXES, shift_pairs(axis_of_core, shift))]
    psum x1 -> x0, blocking collectives: 44.1 us -> none  [on_device(): gradient = lax.psum(partial_grad, 'dp')]
    dot_general x3 -> x0, matrix products: 37.9 us -> none  [the longest x1 13.6 us: on_device(): lax.dot_general(key_grads, piece, (((1,), (1,)), ((), ())), preferred_ele...]
  transfers between devices with their start and end apart: 4 -> 33, of which waited for: 4 -> 8; matrix products, arithmetic and copies ran while one was open for 5% -> 3% of each run, Pallas kernels for 0% -> 13%
where the time goes in v1:
time: 357 us
  Pallas kernels  186 us (52%)
  waiting for transfers between devices  65.2 us (18%)
  starting transfers between devices  64.2 us (18%)
  blocking collectives  24.9 us (7%)
  other arithmetic  8.83 us (2%)
  local copies, waits for them, and re-layouts  6.74 us (2%)
    pallas_call x1, Pallas kernels, split_tokens(): pl.pallas_call(split_kernel, out_shape=jax.ShapeDtypeStruct((TOK, D // 2...  137 us
    ppermute x33, waiting for transfers between devices, send(): return lax.ppermute(array, AXES, shift_pairs(axis_of_core, shift))  65.2 us
    ppermute x33, starting transfers between devices, send(): return lax.ppermute(array, AXES, shift_pairs(axis_of_core, shift))  64.2 us
    all_to_all x1, blocking collectives, on_device(): lax.all_to_all(packed, 'fsdp', split_axis=0, concat_axis=0, tiled=True)  24.9 us
    pallas_call x1, Pallas kernels, gradient_terms(): pl.pallas_call(gradient_kernel, out_shape=(big,) * 4 + (small,) * 2, in_s...  23.3 us
    pallas_call x1, Pallas kernels, final_products(): pl.pallas_call(final_kernel, out_shape=(jax.ShapeDtypeStruct((TOK, C), bf...  20.6 us
  transfers between devices with their start and end apart: 33, of which 8 were waited for; matrix products, arithmetic and copies ran while one was open for 3% of the time, Pallas kernels for 13%

profile of v1, /device:TPU:1, one launch (start us, length us, event | category | flops | bytes accessed | tf_op | source)
XLA Modules:
  0.0 356.7 jit_solution(5914350032938373995)
XLA Ops:
  1.4 137.2 %shard_map.104 = bf16[256,8704]{1,0:T(8,128)(2,1)} custom-call(s32[5]{0:T(128)} %stack.86.place, bf16[256,16384]{1,0:T(8,128)(2,1)} %tokens.5, bf16[256,512]{1,0:T(8,128)(2,1)} %key_grads.5), custom_call_target="tpu_custom_call" | custom-call | bytes 8388608 | tf_op jit(solution)/shard_map/pallas_call | solution.py:85
  138.6 1.5 collective-permute-start.17
  141.4 1.6 copy-done.2
  144.0 24.9 %all_to_all.11 = bf16[32,32,512]{2,1,0:T(8,128)(2,1)S(1)} all-to-all(bf16[32,32,512]{2,1,0:T(8,128)(2,1)S(1)} %bitcast.102), channel_id=1, replica_groups=mesh['fsdp'=32,'dp'=4] {'fsdp'}, dimensions={0} | all-to-all | bytes 2097152 | tf_op jit(solution)/shard_map/all_to_all | solution.py:447
  170.3 1.6 collective-permute-start.1
  172.7 23.3 %shard_map.105 = (bf16[2,4,352,256]{3,2,1,0:T(8,128)(2,1)S(1)}, bf16[2,4,352,256]{3,2,1,0:T(8,128)(2,1)S(1)}, bf16[2,4,352,256]{3,2,1,0:T(8,128)(2,1)S(1)}, bf16...) custom-call(s32[5]{0:T(128)S(1)} %copy-done.5, ...), custom_call_target="tpu_custom_call" | custom-call | flops 4294967296 | bytes 16777216 | tf_op jit(solution)/shard_map/pallas_call | solution.py:222
  196.3 1.2 collective-permute-start.19
  198.7 1.9 collective-permute-start.9
  200.7 13.5 %collective-permute-done.20 = bf16[2,4,352,256]{3,2,1,0:T(8,128)(2,1)S(1)} collective-permute-done((bf16[2,4,352,256]{3,2,1,0:T(8,128)(2,1)S(1)}, bf16[2,4,352,256]{3,2,1,0:T(8,128)(2,1)S(1)}, u32[]{:S(2)}, u32[]{:S(2)}) %collective-permute-start.20) | collective-permute-done | bytes 1441824 | tf_op jit(solution)/shard_map/ppermute | solution.py:57
  214.2 15.2 %collective-permute-start.8 = (bf16[4,160,256]{2,1,0:T(8,128)(2,1)S(1)}, bf16[4,160,256]{2,1,0:T(8,128)(2,1)S(1)}, u32[]{:S(2)}, u32[]{:S(2)}) collective-permute-start(bf16[4,160,256]{2,1,0:T(8,128)(2,1)S(1)} %get-tuple-element.52), channel_id=1, source_target_pairs={{0,8},{1,33},{2,10},{3,35},{64,72},{65,97},{66,74},{67,99},{16,24}... | collective-permute-start | bytes 983048 | tf_op jit(solution)/shard_map/ppermute | solution.py:57
  229.4 5.3 %collective-permute-done.19 = bf16[2,4,352,256]{3,2,1,0:T(8,128)(2,1)S(1)} collective-permute-done((bf16[2,4,352,256]{3,2,1,0:T(8,128)(2,1)S(1)}, bf16[2,4,352,256]{3,2,1,0:T(8,128)(2,1)S(1)}, u32[]{:S(2)}, u32[]{:S(2)}) %collective-permute-start.19) | collective-permute-done | bytes 1441824 | tf_op jit(solution)/shard_map/ppermute | solution.py:57
  235.7 3.4 collective-permute-start.30
  239.7 2.7 collective-permute-start.25
  242.7 14.2 %collective-permute-done.30 = bf16[512,256]{1,0:T(8,128)(2,1)S(1)} collective-permute-done((bf16[512,256]{1,0:T(8,128)(2,1)S(1)}, bf16[512,256]{1,0:T(8,128)(2,1)S(1)}, u32[]{:S(2)}, u32[]{:S(2)}) %collective-permute-start.30) | collective-permute-done | bytes 262176 | tf_op jit(solution)/shard_map/ppermute | solution.py:57
  257.5 3.0 collective-permute-start.4
  261.2 3.5 collective-permute-done.23
  264.7 9.8 %collective-permute-start.15 = (bf16[4,4,160,256]{3,2,1,0:T(8,128)(2,1)S(1)}, bf16[4,4,160,256]{3,2,1,0:T(8,128)(2,1)S(1)}, u32[]{:S(2)}, u32[]{:S(2)}) collective-permute-start(bf16[4,4,160,256]{3,2,1,0:T(8,128)(2,1)S(1)} %pad_maximum_fusion.1.refs_4_), channel_id=1, source_target_pairs={{0,1},{1,0},{2,3},{3,2},{64,65},{65,64},{66,67},{67,66},{16,17},{1... | collective-permute-start | bytes 3932168 | tf_op jit(solution)/shard_map/ppermute | solution.py:57
  274.5 2.5 collective-permute-start.6
  280.2 17.9 %collective-permute-done.10.refs_5_ = bf16[4,4,160,256]{3,2,1,0:T(8,128)(2,1)S(1)} collective-permute-done((bf16[4,4,160,256]{3,2,1,0:T(8,128)(2,1)S(1)}, bf16[4,4,160,256]{3,2,1,0:T(8,128)(2,1)S(1)}, u32[]{:S(2)}, u32[]{:S(2)}) %collective-permute-start.10) | collective-permute-done | bytes 1310752 | tf_op jit(solution)/shard_map/ppermute | solution.py:57
  298.1 4.2 %collective-permute-start.11 = (bf16[2,4,352,256]{3,2,1,0:T(8,128)(2,1)S(1)}, bf16[2,4,352,256]{3,2,1,0:T(8,128)(2,1)}, u32[]{:S(2)}, u32[]{:S(2)}) collective-permute-start(bf16[2,4,352,256]{3,2,1,0:T(8,128)(2,1)S(1)} %pad_maximum_fusion.refs_0_), channel_id=1, source_target_pairs={{0,1},{1,0},{2,3},{3,2},{64,65},{65,64},{66,67},{67,66},{16,17},{1... | collective-permute-start | bytes 4325384 | tf_op jit(solution)/shard_map/ppermute | solution.py:57
  303.2 2.4 collective-permute-start.28
  305.7 1.3 collective-permute-start.26
  307.0 1.7 collective-permute-start.16
  309.3 1.3 collective-permute-start.12
  310.5 5.0 %collective-permute-done.27 = bf16[512,256]{1,0:T(8,128)(2,1)} collective-permute-done((bf16[512,256]{1,0:T(8,128)(2,1)}, bf16[512,256]{1,0:T(8,128)(2,1)}, u32[]{:S(2)}, u32[]{:S(2)}) %collective-permute-start.27) | collective-permute-done | bytes 262176 | tf_op jit(solution)/shard_map/ppermute | solution.py:57
  315.5 1.5 collective-permute-start.13
  318.2 1.4 add_convert_fusion.5
  319.5 3.4 collective-permute-start.29
  323.9 5.3 %collective-permute-done.29 = bf16[512,256]{1,0:T(8,128)(2,1)S(1)} collective-permute-done((bf16[512,256]{1,0:T(8,128)(2,1)S(1)}, bf16[512,256]{1,0:T(8,128)(2,1)S(1)}, u32[]{:S(2)}, u32[]{:S(2)}) %collective-permute-start.29) | collective-permute-done | bytes 262176 | tf_op jit(solution)/shard_map/ppermute | solution.py:57
  332.0 1.1 copy-done.16
  333.1 20.6 %shard_map.103 = (bf16[256,512]{1,0:T(8,128)(2,1)}, bf16[256,16384]{1,0:T(8,128)(2,1)}) custom-call(s32[5]{0:T(128)S(1)} %copy-done.5, bf16[256,16384]{1,0:T(8,128)(2,1)} %tokens.5, bf16[256,512]{1,0:T(8,128)(2,1)S(1)} %copy-done.4, bf16[2,4,352,256]{3,2,1,0:T(8,128)(2,1)S(1)} %pad_maximum_fusion.refs_0_, ...), custom_call_target="tpu_custom_call" | custom-call | flops 8589934592 | bytes 33554432 | tf_op jit(solution)/shard_map/pallas_call | solution.py:317
  353.7 3.1 shard_map.106
  (112 shorter events, 19.4 us)
Async XLA Ops:
  138.6 34.1 %collective-permute-start.17 = (bf16[256,8704]{1,0:T(8,128)(2,1)}, bf16[256,8704]{1,0:T(8,128)(2,1)}, u32[]{:S(2)}, u32[]{:S(2)}) collective-permute-start(bf16[256,8704]{1,0:T(8,128)(2,1)} %shard_map.104), channel_id=1, source_target_pairs={{0,1},{1,0},{2,3},{3,2},{64,65},{65,64},{66,67},{67,66},{16,17},{1... | collective-permute-start | bytes 13369352 | tf_op jit(solution)/shard_map/ppermute | solution.py:57
  169.5 28.0 %collective-permute-start.2 = (bf16[512,256]{1,0:T(8,128)(2,1)S(1)}, bf16[512,256]{1,0:T(8,128)(2,1)S(1)}, u32[]{:S(2)}, u32[]{:S(2)}) collective-permute-start(bf16[512,256]{1,0:T(8,128)(2,1)S(1)} %get-tuple-element.18.weights), channel_id=1, source_target_pairs={{0,48},{1,13},{2,50},{3,15},{64,112},{65,77},{66,114},{67,79},{16,... | collective-permute-start | bytes 786440 | tf_op jit(solution)/shard_map/ppermute | solution.py:57
  170.3 27.7 %collective-permute-start.1 = (bf16[512,256]{1,0:T(8,128)(2,1)S(1)}, bf16[512,256]{1,0:T(8,128)(2,1)S(1)}, u32[]{:S(2)}, u32[]{:S(2)}) collective-permute-start(bf16[512,256]{1,0:T(8,128)(2,1)S(1)} %get-tuple-element.18.weights), channel_id=1, source_target_pairs={{0,32},{1,9},{2,34},{3,11},{64,96},{65,73},{66,98},{67,75},{16,48}... | collective-permute-start | bytes 786440 | tf_op jit(solution)/shard_map/ppermute | solution.py:57
  171.8 26.7 %collective-permute-start = (bf16[512,256]{1,0:T(8,128)(2,1)S(1)}, bf16[512,256]{1,0:T(8,128)(2,1)S(1)}, u32[]{:S(2)}, u32[]{:S(2)}) collective-permute-start(bf16[512,256]{1,0:T(8,128)(2,1)S(1)} %get-tuple-element.18.weights), channel_id=1, source_target_pairs={{0,16},{1,5},{2,18},{3,7},{64,80},{65,69},{66,82},{67,71},{16,32},... | collective-permute-start | bytes 786440 | tf_op jit(solution)/shard_map/ppermute | solution.py:57
  196.0 18.2 %collective-permute-start.20 = (bf16[2,4,352,256]{3,2,1,0:T(8,128)(2,1)S(1)}, bf16[2,4,352,256]{3,2,1,0:T(8,128)(2,1)S(1)}, u32[]{:S(2)}, u32[]{:S(2)}) collective-permute-start(bf16[2,4,352,256]{3,2,1,0:T(8,128)(2,1)S(1)} %get-tuple-element.24), channel_id=1, source_target_pairs={{0,12},{1,49},{2,14},{3,51},{64,76},{65,113},{66,78},{67,115},{16,... | collective-permute-start | bytes 4325384 | tf_op jit(solution)/shard_map/ppermute | solution.py:57
  196.3 38.3 %collective-permute-start.19 = (bf16[2,4,352,256]{3,2,1,0:T(8,128)(2,1)S(1)}, bf16[2,4,352,256]{3,2,1,0:T(8,128)(2,1)S(1)}, u32[]{:S(2)}, u32[]{:S(2)}) collective-permute-start(bf16[2,4,352,256]{3,2,1,0:T(8,128)(2,1)S(1)} %get-tuple-element.23), channel_id=1, source_target_pairs={{0,4},{1,17},{2,6},{3,19},{64,68},{65,81},{66,70},{67,83},{16,20},... | collective-permute-start | bytes 4325384 | tf_op jit(solution)/shard_map/ppermute | solution.py:57
  197.5 37.2 %collective-permute-start.18 = (bf16[2,4,352,256]{3,2,1,0:T(8,128)(2,1)S(1)}, bf16[2,4,352,256]{3,2,1,0:T(8,128)(2,1)S(1)}, u32[]{:S(2)}, u32[]{:S(2)}) collective-permute-start(bf16[2,4,352,256]{3,2,1,0:T(8,128)(2,1)S(1)} %get-tuple-element.22), channel_id=1, source_target_pairs={{0,8},{1,33},{2,10},{3,35},{64,72},{65,97},{66,74},{67,99},{16,24}... | collective-permute-start | bytes 4325384 | tf_op jit(solution)/shard_map/ppermute | solution.py:57
  198.0 41.1 %collective-permute-start.22 = (bf16[4,4,160,256]{3,2,1,0:T(8,128)(2,1)S(1)}, bf16[4,4,160,256]{3,2,1,0:T(8,128)(2,1)S(1)}, u32[]{:S(2)}, u32[]{:S(2)}) collective-permute-start(bf16[4,4,160,256]{3,2,1,0:T(8,128)(2,1)S(1)} %get-tuple-element.26), channel_id=1, source_target_pairs={{0,64},{1,65},{2,66},{3,67},{64,0},{65,1},{66,2},{67,3},{16,80},{1... | collective-permute-start | bytes 3932168 | tf_op jit(solution)/shard_map/ppermute | solution.py:57
  198.7 37.1 %collective-permute-start.9 = (bf16[4,160,256]{2,1,0:T(8,128)(2,1)S(1)}, bf16[4,160,256]{2,1,0:T(8,128)(2,1)S(1)}, u32[]{:S(2)}, u32[]{:S(2)}) collective-permute-start(bf16[4,160,256]{2,1,0:T(8,128)(2,1)S(1)} %get-tuple-element.52), channel_id=1, source_target_pairs={{0,12},{1,49},{2,14},{3,51},{64,76},{65,113},{66,78},{67,115},{16,... | collective-permute-start | bytes 983048 | tf_op jit(solution)/shard_map/ppermute | solution.py:57
  214.2 25.5 %collective-permute-start.8 = (bf16[4,160,256]{2,1,0:T(8,128)(2,1)S(1)}, bf16[4,160,256]{2,1,0:T(8,128)(2,1)S(1)}, u32[]{:S(2)}, u32[]{:S(2)}) collective-permute-start(bf16[4,160,256]{2,1,0:T(8,128)(2,1)S(1)} %get-tuple-element.52), channel_id=1, source_target_pairs={{0,8},{1,33},{2,10},{3,35},{64,72},{65,97},{66,74},{67,99},{16,24}... | collective-permute-start | bytes 983048 | tf_op jit(solution)/shard_map/ppermute | solution.py:57
  234.7 7.8 %collective-permute-start.7 = (bf16[4,160,256]{2,1,0:T(8,128)(2,1)S(1)}, bf16[4,160,256]{2,1,0:T(8,128)(2,1)S(1)}, u32[]{:S(2)}, u32[]{:S(2)}) collective-permute-start(bf16[4,160,256]{2,1,0:T(8,128)(2,1)S(1)} %get-tuple-element.52), channel_id=1, source_target_pairs={{0,4},{1,17},{2,6},{3,19},{64,68},{65,81},{66,70},{67,83},{16,20},... | collective-permute-start | bytes 983048 | tf_op jit(solution)/shard_map/ppermute | solution.py:57
  234.7 22.2 %collective-permute-start.3 = (bf16[4,352,256]{2,1,0:T(8,128)(2,1)S(1)}, bf16[4,352,256]{2,1,0:T(8,128)(2,1)S(1)}, u32[]{:S(2)}, u32[]{:S(2)}) collective-permute-start(bf16[4,352,256]{2,1,0:T(8,128)(2,1)S(1)} %get-tuple-element.46), channel_id=1, source_target_pairs={{0,64},{1,65},{2,66},{3,67},{64,0},{65,1},{66,2},{67,3},{16,80},{1... | collective-permute-start | bytes 2162696 | tf_op jit(solution)/shard_map/ppermute | solution.py:57
  235.7 21.1 %collective-permute-start.30 = (bf16[512,256]{1,0:T(8,128)(2,1)S(1)}, bf16[512,256]{1,0:T(8,128)(2,1)S(1)}, u32[]{:S(2)}, u32[]{:S(2)}) collective-permute-start(bf16[512,256]{1,0:T(8,128)(2,1)S(1)} %get-tuple-element.27), channel_id=1, source_target_pairs={{0,2},{1,3},{2,0},{3,1},{64,66},{65,67},{66,64},{67,65},{16,18},{1... | collective-permute-start | bytes 786440 | tf_op jit(solution)/shard_map/ppermute | solution.py:57
  239.1 35.3 %collective-permute-start.21 = (bf16[4,352,256]{2,1,0:T(8,128)(2,1)S(1)}, bf16[4,352,256]{2,1,0:T(8,128)(2,1)S(1)}, u32[]{:S(2)}, u32[]{:S(2)}) collective-permute-start(bf16[4,352,256]{2,1,0:T(8,128)(2,1)S(1)} %fusion), channel_id=1, source_target_pairs={{0,64},{1,65},{2,66},{3,67},{64,0},{65,1},{66,2},{67,3},{16,80},{1... | collective-permute-start | bytes 2162696 | tf_op jit(solution)/shard_map/ppermute | solution.py:57
  239.7 17.8 %collective-permute-start.25 = (bf16[4,160,256]{2,1,0:T(8,128)(2,1)S(1)}, bf16[4,160,256]{2,1,0:T(8,128)(2,1)S(1)}, u32[]{:S(2)}, u32[]{:S(2)}) collective-permute-start(bf16[4,160,256]{2,1,0:T(8,128)(2,1)S(1)} %get-tuple-element.38), channel_id=1, source_target_pairs={{0,12},{1,49},{2,14},{3,51},{64,76},{65,113},{66,78},{67,115},{16,... | collective-permute-start | bytes 983048 | tf_op jit(solution)/shard_map/ppermute | solution.py:57
  242.5 18.1 %collective-permute-start.24 = (bf16[4,160,256]{2,1,0:T(8,128)(2,1)S(1)}, bf16[4,160,256]{2,1,0:T(8,128)(2,1)S(1)}, u32[]{:S(2)}, u32[]{:S(2)}) collective-permute-start(bf16[4,160,256]{2,1,0:T(8,128)(2,1)S(1)} %get-tuple-element.39), channel_id=1, source_target_pairs={{0,4},{1,17},{2,6},{3,19},{64,68},{65,81},{66,70},{67,83},{16,20},... | collective-permute-start | bytes 983048 | tf_op jit(solution)/shard_map/ppermute | solution.py:57
  256.8 41.3 %collective-permute-start.10 = (bf16[4,4,160,256]{3,2,1,0:T(8,128)(2,1)S(1)}, bf16[4,4,160,256]{3,2,1,0:T(8,128)(2,1)S(1)}, u32[]{:S(2)}, u32[]{:S(2)}) collective-permute-start(bf16[4,4,160,256]{3,2,1,0:T(8,128)(2,1)S(1)} %pad_maximum_fusion.1.refs_4_), channel_id=1, source_target_pairs={{0,64},{1,65},{2,66},{3,67},{64,0},{65,1},{66,2},{67,3},{16,80},{1... | collective-permute-start | bytes 3932168 | tf_op jit(solution)/shard_map/ppermute | solution.py:57
  256.9 7.8 %collective-permute-start.23 = (bf16[4,160,256]{2,1,0:T(8,128)(2,1)S(1)}, bf16[4,160,256]{2,1,0:T(8,128)(2,1)S(1)}, u32[]{:S(2)}, u32[]{:S(2)}) collective-permute-start(bf16[4,160,256]{2,1,0:T(8,128)(2,1)S(1)} %get-tuple-element.40), channel_id=1, source_target_pairs={{0,8},{1,33},{2,10},{3,35},{64,72},{65,97},{66,74},{67,99},{16,24}... | collective-permute-start | bytes 983048 | tf_op jit(solution)/shard_map/ppermute | solution.py:57
  257.5 48.1 %collective-permute-start.4 = (bf16[2,4,352,256]{3,2,1,0:T(8,128)(2,1)S(1)}, bf16[2,4,352,256]{3,2,1,0:T(8,128)(2,1)}, u32[]{:S(2)}, u32[]{:S(2)}) collective-permute-start(bf16[2,4,352,256]{3,2,1,0:T(8,128)(2,1)S(1)} %pad_maximum_fusion.refs_0_), channel_id=1, source_target_pairs={{0,4},{1,17},{2,6},{3,19},{64,68},{65,81},{66,70},{67,83},{16,20},... | collective-permute-start | bytes 4325384 | tf_op jit(solution)/shard_map/ppermute | solution.py:57
  260.6 45.1 %collective-permute-start.5 = (bf16[2,4,352,256]{3,2,1,0:T(8,128)(2,1)S(1)}, bf16[2,4,352,256]{3,2,1,0:T(8,128)(2,1)}, u32[]{:S(2)}, u32[]{:S(2)}) collective-permute-start(bf16[2,4,352,256]{3,2,1,0:T(8,128)(2,1)S(1)} %pad_maximum_fusion.refs_0_), channel_id=1, source_target_pairs={{0,8},{1,33},{2,10},{3,35},{64,72},{65,97},{66,74},{67,99},{16,24}... | collective-permute-start | bytes 4325384 | tf_op jit(solution)/shard_map/ppermute | solution.py:57
  264.7 38.6 %collective-permute-start.15 = (bf16[4,4,160,256]{3,2,1,0:T(8,128)(2,1)S(1)}, bf16[4,4,160,256]{3,2,1,0:T(8,128)(2,1)S(1)}, u32[]{:S(2)}, u32[]{:S(2)}) collective-permute-start(bf16[4,4,160,256]{3,2,1,0:T(8,128)(2,1)S(1)} %pad_maximum_fusion.1.refs_4_), channel_id=1, source_target_pairs={{0,1},{1,0},{2,3},{3,2},{64,65},{65,64},{66,67},{67,66},{16,17},{1... | collective-permute-start | bytes 3932168 | tf_op jit(solution)/shard_map/ppermute | solution.py:57
  274.5 32.5 %collective-permute-start.6 = (bf16[2,4,352,256]{3,2,1,0:T(8,128)(2,1)S(1)}, bf16[2,4,352,256]{3,2,1,0:T(8,128)(2,1)}, u32[]{:S(2)}, u32[]{:S(2)}) collective-permute-start(bf16[2,4,352,256]{3,2,1,0:T(8,128)(2,1)S(1)} %pad_maximum_fusion.refs_0_), channel_id=1, source_target_pairs={{0,12},{1,49},{2,14},{3,51},{64,76},{65,113},{66,78},{67,115},{16,... | collective-permute-start | bytes 4325384 | tf_op jit(solution)/shard_map/ppermute | solution.py:57
  298.1 21.4 %collective-permute-start.11 = (bf16[2,4,352,256]{3,2,1,0:T(8,128)(2,1)S(1)}, bf16[2,4,352,256]{3,2,1,0:T(8,128)(2,1)}, u32[]{:S(2)}, u32[]{:S(2)}) collective-permute-start(bf16[2,4,352,256]{3,2,1,0:T(8,128)(2,1)S(1)} %pad_maximum_fusion.refs_0_), channel_id=1, source_target_pairs={{0,1},{1,0},{2,3},{3,2},{64,65},{65,64},{66,67},{67,66},{16,17},{1... | collective-permute-start | bytes 4325384 | tf_op jit(solution)/shard_map/ppermute | solution.py:57
  305.6 9.9 %collective-permute-start.27 = (bf16[512,256]{1,0:T(8,128)(2,1)}, bf16[512,256]{1,0:T(8,128)(2,1)}, u32[]{:S(2)}, u32[]{:S(2)}) collective-permute-start(bf16[512,256]{1,0:T(8,128)(2,1)} %pad_maximum_fusion.6), channel_id=1, source_target_pairs={{0,16},{1,5},{2,18},{3,7},{64,80},{65,69},{66,82},{67,71},{16,32},... | collective-permute-start | bytes 786440 | tf_op jit(solution)/shard_map/ppermute | solution.py:57
  305.7 11.4 %collective-permute-start.26 = (bf16[512,256]{1,0:T(8,128)(2,1)}, bf16[512,256]{1,0:T(8,128)(2,1)}, u32[]{:S(2)}, u32[]{:S(2)}) collective-permute-start(bf16[512,256]{1,0:T(8,128)(2,1)} %pad_maximum_fusion.5), channel_id=1, source_target_pairs={{0,32},{1,9},{2,34},{3,11},{64,96},{65,73},{66,98},{67,75},{16,48}... | collective-permute-start | bytes 786440 | tf_op jit(solution)/shard_map/ppermute | solution.py:57
  307.0 23.3 %collective-permute-start.16 = (bf16[4,4,160,256]{3,2,1,0:T(8,128)(2,1)}, bf16[4,4,160,256]{3,2,1,0:T(8,128)(2,1)S(1)}, u32[]{:S(2)}, u32[]{:S(2)}) collective-permute-start(bf16[4,4,160,256]{3,2,1,0:T(8,128)(2,1)} %copy-done.8), channel_id=1, source_target_pairs={{0,1},{1,0},{2,3},{3,2},{64,65},{65,64},{66,67},{67,66},{16,17},{1... | collective-permute-start | bytes 3932168 | tf_op jit(solution)/shard_map/ppermute | solution.py:57
  309.3 21.1 %collective-permute-start.12 = (bf16[2,4,352,256]{3,2,1,0:T(8,128)(2,1)}, bf16[2,4,352,256]{3,2,1,0:T(8,128)(2,1)S(1)}, u32[]{:S(2)}, u32[]{:S(2)}) collective-permute-start(bf16[2,4,352,256]{3,2,1,0:T(8,128)(2,1)} %collective-permute-done.4.refs_1_), channel_id=1, source_target_pairs={{0,1},{1,0},{2,3},{3,2},{64,65},{65,64},{66,67},{67,66},{16,17},{1... | collective-permute-start | bytes 4325384 | tf_op jit(solution)/shard_map/ppermute | solution.py:57
  315.5 14.9 %collective-permute-start.13 = (bf16[2,4,352,256]{3,2,1,0:T(8,128)(2,1)}, bf16[2,4,352,256]{3,2,1,0:T(8,128)(2,1)S(1)}, u32[]{:S(2)}, u32[]{:S(2)}) collective-permute-start(bf16[2,4,352,256]{3,2,1,0:T(8,128)(2,1)} %collective-permute-done.5.refs_2_), channel_id=1, source_target_pairs={{0,1},{1,0},{2,3},{3,2},{64,65},{65,64},{66,67},{67,66},{16,17},{1... | collective-permute-start | bytes 4325384 | tf_op jit(solution)/shard_map/ppermute | solution.py:57
  317.0 13.4 %collective-permute-start.14 = (bf16[2,4,352,256]{3,2,1,0:T(8,128)(2,1)}, bf16[2,4,352,256]{3,2,1,0:T(8,128)(2,1)S(1)}, u32[]{:S(2)}, u32[]{:S(2)}) collective-permute-start(bf16[2,4,352,256]{3,2,1,0:T(8,128)(2,1)} %collective-permute-done.6.refs_3_), channel_id=1, source_target_pairs={{0,1},{1,0},{2,3},{3,2},{64,65},{65,64},{66,67},{67,66},{16,17},{1... | collective-permute-start | bytes 4325384 | tf_op jit(solution)/shard_map/ppermute | solution.py:57
  319.5 9.6 %collective-permute-start.29 = (bf16[512,256]{1,0:T(8,128)(2,1)S(1)}, bf16[512,256]{1,0:T(8,128)(2,1)S(1)}, u32[]{:S(2)}, u32[]{:S(2)}) collective-permute-start(bf16[512,256]{1,0:T(8,128)(2,1)S(1)} %add_convert_fusion.5), channel_id=1, source_target_pairs={{0,2},{1,3},{2,0},{3,1},{64,66},{65,67},{66,64},{67,65},{16,18},{1... | collective-permute-start | bytes 786440 | tf_op jit(solution)/shard_map/ppermute | solution.py:57
  329.1 24.5 %collective-permute-start.32 = (bf16[512,512]{1,0:T(8,128)(2,1)S(1)}, bf16[512,512]{1,0:T(8,128)(2,1)S(1)}, u32[]{:S(2)}, u32[]{:S(2)}) collective-permute-start(bf16[512,512]{1,0:T(8,128)(2,1)S(1)} %pad_maximum_fusion.3.moments), channel_id=1, source_target_pairs={{0,1},{1,0},{2,3},{3,2},{64,65},{65,64},{66,67},{67,66},{16,17},{1... | collective-permute-start | bytes 1572872 | tf_op jit(solution)/shard_map/ppermute | solution.py:57
  330.3 23.4 %collective-permute-start.31 = (f32[512,256]{1,0:T(8,128)S(1)}, f32[512,256]{1,0:T(8,128)S(1)}, u32[]{:S(2)}, u32[]{:S(2)}) collective-permute-start(f32[512,256]{1,0:T(8,128)S(1)} %convert_add_fusion.grads), channel_id=1, source_target_pairs={{0,1},{1,0},{2,3},{3,2},{64,65},{65,64},{66,67},{67,66},{16,17},{1... | collective-permute-start | bytes 1572872 | tf_op jit(solution)/shard_map/ppermute | solution.py:57
  (18 other events, 687.5 us)

commit v2 on v1

v2 whole, which is shorter than its diff:
```python
import functools
import itertools

import jax
import jax.numpy as jnp
from jax import lax
from jax.experimental import pallas as pl
from jax.experimental.pallas import tpu as pltpu
from jax.sharding import PartitionSpec as P

BR = 16
C = 512
HALF = 256
QUARTER = 128
TOK = 256
D = 16384
NF = 32

beta_first = 0.9
beta_second = 0.95
eps_adam = 1e-08
learn_rate = 0.001
decay_rate = 0.1
bias_first = 1.0 - 0.9**10
bias_second = 1.0 - 0.95**10

AXES = ("fsdp", "dp")
bf16 = jnp.bfloat16
f32 = jnp.float32
ANY = pl.BlockSpec(memory_space=pl.ANY)
SMEM = pl.BlockSpec(memory_space=pltpu.SMEM)
VMEM = pl.BlockSpec(memory_space=pltpu.VMEM)
LIGHT = pl.CostEstimate(flops=0, bytes_accessed=1024, transcendentals=0)


def device_number(x, y, zl, zh, core):
    return (((zl * 4 + y) * 4 + x) * 2 + zh) * 2 + core


def shift_pairs(axis_of_core, shift):
    pairs = []
    for x, y, zl, zh, core in itertools.product(range(4), range(4), range(2), range(2), range(2)):
        to = {"x": x, "y": y, "l": zl, "h": zh, "c": core}
        axis = axis_of_core[core]
        to[axis] = (to[axis] + shift) % (4 if axis in "xy" else 2)
        pairs.append(
            (
                device_number(x, y, zl, zh, core),
                device_number(to["x"], to["y"], to["l"], to["h"], to["c"]),
            )
        )
    return pairs


def send(array, axis_of_core, shift=1):
    return lax.ppermute(array, AXES, shift_pairs(axis_of_core, shift))


OUTER = "xy"
INNER = "yx"
PAIR = "ll"
REPLICA = "hh"
CORE = "cc"


def split_kernel(place, tokens, key_grads, mine, out):
    core = place[3]
    for i in range(NF):
        at = lambda k: pl.ds(pl.multiple_of(i * C + k * HALF, HALF), HALF)
        mine[:, i * HALF : (i + 1) * HALF] = tokens[:, at(core)]
        out[:, i * HALF : (i + 1) * HALF] = tokens[:, at(1 - core)]
    out[:, D // 2 :] = key_grads[...]


def split_tokens(place, tokens, key_grads):
    rows = 32
    band = lambda width: pl.BlockSpec((rows, width), lambda i, place: (i, 0))
    return pl.pallas_call(
        split_kernel,
        out_shape=(
            jax.ShapeDtypeStruct((TOK, D // 2), bf16),
            jax.ShapeDtypeStruct((TOK, D // 2 + C), bf16),
        ),
        grid_spec=pltpu.PrefetchScalarGridSpec(
            num_scalar_prefetch=1,
            grid=(TOK // rows,),
            in_specs=[band(D), band(C)],
            out_specs=(band(D // 2), band(D // 2 + C)),
        ),
        compiler_params=pltpu.CompilerParams(vmem_limit_bytes=54 * 2**20),
        cost_estimate=LIGHT,
    )(place, tokens, key_grads)


def pack_kernel(place, table, param, first, second, out):
    def body(k, carry):
        src = pl.multiple_of(table[k] * BR, BR)
        dst = pl.multiple_of(k * BR, BR)
        out[pl.ds(dst, BR), :HALF] = param[pl.ds(src, BR), :]
        out[pl.ds(dst, BR), HALF : HALF + QUARTER] = first[pl.ds(src, BR), :].astype(bf16)
        out[pl.ds(dst, BR), HALF + QUARTER :] = second[pl.ds(src, BR), :].astype(bf16)
        return carry

    lax.fori_loop(0, 2 * NF, body, 0, unroll=4)


def pack(place, table, param, first, second):
    rows = param.shape[0]
    quarter = lambda i, place, table: (0, place[3] * 2 + place[4])
    return pl.pallas_call(
        pack_kernel,
        out_shape=jax.ShapeDtypeStruct((2 * NF * BR, C), bf16),
        grid_spec=pltpu.PrefetchScalarGridSpec(
            num_scalar_prefetch=2,
            grid=(1,),
            in_specs=[
                pl.BlockSpec((rows, HALF), lambda i, place, table: (0, place[3])),
                pl.BlockSpec((rows, QUARTER), quarter),
                pl.BlockSpec((rows, QUARTER), quarter),
            ],
            out_specs=pl.BlockSpec((2 * NF * BR, C), lambda i, place, table: (0, 0)),
        ),
        compiler_params=pltpu.CompilerParams(vmem_limit_bytes=2**24),
        cost_estimate=LIGHT,
    )(place, table, param, first, second)


def unpack_kernel(rows_taken, got, weight, moments):
    def body(k, carry):
        src = pl.multiple_of(rows_taken[k] * BR, BR)
        dst = pl.multiple_of(k * BR, BR)
        weight[pl.ds(dst, BR), :] = got[pl.ds(src, BR), :HALF]
        moments[pl.ds(dst, BR), :] = got[pl.ds(src, BR), HALF:]
        return carry

    lax.fori_loop(0, NF, body, 0, unroll=4)


def unpack(rows_taken, got):
    half = jax.ShapeDtypeStruct((C, HALF), bf16)
    return pl.pallas_call(
        unpack_kernel,
        out_shape=(half, half),
        in_specs=[SMEM, VMEM],
        out_specs=(VMEM, VMEM),
        compiler_params=pltpu.CompilerParams(vmem_limit_bytes=2**23),
        cost_estimate=LIGHT,
    )(rows_taken, got)


def target_index(place, core, outer, pair, inner, sign):
    x, y, zl = place[0], place[1], place[2]
    along_x = jnp.where(core == 0, outer, inner)
    along_y = jnp.where(core == 0, inner, outer)
    to_x = lax.rem(x + sign * along_x + 4, 4)
    to_y = lax.rem(y + sign * along_y + 4, 4)
    to_z = lax.rem(zl + pair, 2)
    return (to_z * 4 + to_y) * 4 + to_x


def gradient_term(place, mine, theirs, grads_t, outer, inner, pair):
    core = place[3]
    f = target_index(place, core, outer, pair, inner, 1)
    at = pl.ds(pl.multiple_of(f * HALF, HALF), HALF)
    return jnp.dot(
        grads_t[...],
        jnp.concatenate([mine[:, at], theirs[:, at]], axis=0),
        preferred_element_type=f32,
    ).astype(bf16)


def far_gradient_kernel(place, mine, theirs, key_grads, plus, minus, grads_t):
    grads_t[:, :TOK] = key_grads[...].T
    grads_t[:, TOK:] = theirs[:, D // 2 :].T
    for inner in range(2):
        for pair in range(2):
            term = functools.partial(gradient_term, place, mine, theirs, grads_t, 2)
            plus[inner, pair] = term(inner, pair)
            minus[inner, pair] = term(inner + 2, pair)


def near_gradient_kernel(place, mine, theirs, grads_t, *refs):
    for ref, (outer, first) in zip(refs, ((1, 2), (3, 0), (1, 0), (3, 2), (0, 0), (0, 2))):

        def body(inner, carry, ref=ref, outer=outer, first=first):
            for pair in range(2):
                ref[inner, pair] = gradient_term(
                    place, mine, theirs, grads_t, outer, first + inner, pair
                )
            return carry

        lax.fori_loop(0, 2, body, 0, unroll=2)


def gradient_terms(place, mine, theirs, key_grads):
    half = jax.ShapeDtypeStruct((2, 2, C, HALF), bf16)
    far_plus, far_minus, grads_t = pl.pallas_call(
        far_gradient_kernel,
        out_shape=(half, half, jax.ShapeDtypeStruct((C, 2 * TOK), bf16)),
        in_specs=[SMEM, VMEM, VMEM, VMEM],
        out_specs=(VMEM,) * 3,
        compiler_params=pltpu.CompilerParams(vmem_limit_bytes=20 * 2**20),
        cost_estimate=LIGHT,
    )(place, mine, theirs, key_grads)
    near = pl.pallas_call(
        near_gradient_kernel,
        out_shape=(half,) * 6,
        in_specs=[SMEM, VMEM, VMEM, VMEM],
        out_specs=(VMEM,) * 6,
        compiler_params=pltpu.CompilerParams(vmem_limit_bytes=24 * 2**20),
        cost_estimate=LIGHT,
    )(place, mine, theirs, grads_t)
    return (far_plus, far_minus) + tuple(near)


def is_near(outer, inner):
    return outer != 2 and inner != 2


def products(place, tokens, key_grads, piece, near, total, scratch, input_grads, start):
    held, weights, made, sem_in, sem_w, sem = scratch
    core = place[3]
    turn = lambda k: pl.ds(pl.multiple_of(k * HALF, HALF), HALF)
    steps = [
        (outer, inner, pair)
        for outer in range(4)
        for inner in range(4)
        for pair in range(2)
        if is_near(outer, inner) == near
    ]
    spots, loads = [], []
    for k, (outer, inner, pair) in enumerate(steps):
        f = target_index(place, core, outer, pair, inner, -1)
        spots.append(pl.ds(pl.multiple_of(f * C, C), C))
        sources = (piece(0, outer, inner, pair), piece(1, inner, outer, pair))
        loads.append(
            [
                pltpu.make_async_copy(sources[of], weights.at[k, of], sem_w.at[of, k])
                for of in range(2)
            ]
            + [pltpu.make_async_copy(tokens.at[:, spots[k]], held.at[k], sem_in.at[k])]
        )
        for copy in loads[k]:
            copy.start()
    grads = jnp.concatenate([key_grads[:, turn(core)], key_grads[:, turn(1 - core)]], axis=1)
    for k in range(len(steps)):
        for copy in loads[k]:
            copy.wait()
        weight = jnp.concatenate([weights[k, 0], weights[k, 1]], axis=1)
        made[k] = lax.dot_general(
            grads, weight, (((1,), (1,)), ((), ())), preferred_element_type=f32
        ).astype(bf16)
        pltpu.make_async_copy(made.at[k], input_grads.at[:, spots[k]], sem).start()
        term = jnp.dot(held[k], weight, preferred_element_type=f32)
        if k == 0:
            total[...] = term if start is None else start[...] + term
        else:
            total[...] += term
    pltpu.make_async_copy(made, made, sem).wait()


def piece_of(arrays, per_core):
    which = {0: 0, 1: 1, 3: 2}

    def piece(of, outer, inner, pair):
        if outer == 2:
            return arrays[per_core * of + 3 + inner // 2].at[inner % 2, pair]
        return arrays[per_core * of + which[outer]].at[inner, pair]

    return piece


def near_kernel(place, tokens, key_grads, *refs):
    arrays, (total, input_grads, *scratch) = refs[:6], refs[6:]
    piece = piece_of(arrays, 3)
    products(place, tokens, key_grads, piece, True, total, scratch, input_grads, None)


def far_kernel(place, tokens, key_grads, start, near_grads, *refs):
    arrays, (keys, input_grads, total, *scratch) = refs[:10], refs[10:]
    piece = piece_of(arrays, 5)
    products(place, tokens, key_grads, piece, False, total, scratch, input_grads, start)
    core = place[3]
    for of in range(2):
        owner = core if of == 0 else 1 - core
        keys[:, pl.ds(pl.multiple_of(owner * HALF, HALF), HALF)] = total[
            :, of * HALF : (of + 1) * HALF
        ].astype(bf16)


def product_scratch(steps):
    return [
        pltpu.VMEM((steps, TOK, C), bf16),
        pltpu.VMEM((steps, 2, C, HALF), bf16),
        pltpu.VMEM((steps, TOK, C), bf16),
        pltpu.SemaphoreType.DMA((steps,)),
        pltpu.SemaphoreType.DMA((2, steps)),
        pltpu.SemaphoreType.DMA,
    ]


def near_products(place, tokens, key_grads, pieces):
    return pl.pallas_call(
        near_kernel,
        out_shape=(
            jax.ShapeDtypeStruct((TOK, C), f32),
            jax.ShapeDtypeStruct((TOK, D), bf16),
        ),
        in_specs=[SMEM, ANY, VMEM] + [ANY] * 6,
        out_specs=(VMEM, ANY),
        scratch_shapes=product_scratch(18),
        compiler_params=pltpu.CompilerParams(vmem_limit_bytes=56 * 2**20),
        cost_estimate=LIGHT,
    )(place, tokens, key_grads, *pieces)


def far_products(place, tokens, key_grads, start, near_grads, pieces):
    return pl.pallas_call(
        far_kernel,
        out_shape=(
            jax.ShapeDtypeStruct((TOK, C), bf16),
            jax.ShapeDtypeStruct((TOK, D), bf16),
        ),
        in_specs=[SMEM, ANY, VMEM, VMEM] + [ANY] * 11,
        out_specs=(VMEM, ANY),
        scratch_shapes=[pltpu.VMEM((TOK, C), f32)] + product_scratch(14),
        input_output_aliases={4: 1},
        compiler_params=pltpu.CompilerParams(vmem_limit_bytes=56 * 2**20),
        cost_estimate=LIGHT,
    )(place, tokens, key_grads, start, near_grads, *pieces)


def routes(old_home, f, slots):
    home = old_home.reshape(NF, NF)
    source = home // slots
    idx = jnp.arange(NF)
    earlier = idx[None, :, None] > idx[None, None, :]
    same = source[:, :, None] == source[:, None, :]
    rank = jnp.sum((same & earlier).astype(jnp.int32), axis=2)
    mine = source == f
    slot = jnp.where(mine, home % slots, 0)
    table = jnp.stack([jnp.sum(jnp.where(rank == r, slot, 0), axis=1) for r in range(2)], axis=1)
    arrives = source * 2 + rank
    rows_taken = jnp.sum(jnp.where(idx[:, None] == f, arrives, 0), axis=0)
    return table.reshape(2 * NF), rows_taken


def add(*terms):
    total = terms[0].astype(f32)
    for term in terms[1:]:
        total = total + term.astype(f32)
    return total


def tied(*values):
    return lax.optimization_barrier(values)


def adamw_kernel(place, grads, weights, moments, *refs):
    grads_other, weights_other, moments_other, new_param, new_first, new_second = refs

    def update(core):
        for r in range(2):
            rows = pl.ds(r * HALF, HALF)
            turned = (grads if r == core else grads_other)[...].T
            for c in range(2):
                cols = pl.ds(c * HALF, HALF)
                m = moments if c == core else moments_other
                weight = (weights if c == core else weights_other)[rows, :].astype(f32)
                gradient = turned[:, c * HALF : (c + 1) * HALF]
                first = beta_first * m[rows, :HALF].astype(f32) + (1.0 - beta_first) * gradient
                second = (
                    beta_second * m[rows, HALF:].astype(f32)
                    + (1.0 - beta_second) * gradient * gradient
                )
                step = (
                    first / bias_first / (jnp.sqrt(second / bias_second) + eps_adam)
                    + decay_rate * weight
                )
                new_first[rows, cols] = first
                new_second[rows, cols] = second
                new_param[rows, cols] = (weight - learn_rate * step).astype(bf16)

    for core in range(2):
        pl.when(place[3] == core)(functools.partial(update, core))


def adamw(place, own, other):
    wide = jax.ShapeDtypeStruct((C, C), f32)
    return pl.pallas_call(
        adamw_kernel,
        out_shape=(jax.ShapeDtypeStruct((C, C), bf16), wide, wide),
        in_specs=[SMEM] + [VMEM] * 6,
        out_specs=(VMEM,) * 3,
        compiler_params=pltpu.CompilerParams(vmem_limit_bytes=2**24),
        cost_estimate=LIGHT,
    )(place, *own, *other)


def ordered(index, own, other, axis):
    low = jnp.where(index == 0, own, other)
    high = jnp.where(index == 0, other, own)
    return jnp.concatenate([low, high], axis=axis)


def on_device(tokens, key_grads, old_param, old_first, old_second, old_home):
    f = lax.axis_index("fsdp").astype(jnp.int32)
    d = lax.axis_index("dp").astype(jnp.int32)
    core, zh = d % 2, d // 2
    place = jnp.stack([f % 4, (f // 4) % 4, f // 16, core, zh])

    mine, for_other = split_tokens(place, tokens, key_grads)
    terms = gradient_terms(place, mine, send(for_other, CORE), key_grads)
    far_plus, far_minus, plus_b, minus_a, plus_a, minus_b, stay_a, stay_b = terms

    table, rows_taken = routes(old_home, f, old_param.shape[0] // BR)
    packed = pack(place, table, old_param, old_first, old_second)

    far_plus, far_minus = send(far_plus, OUTER, 1), send(far_minus, OUTER, 3)
    plus_a = add(plus_a, far_plus).astype(bf16)
    minus_b = add(minus_b, far_minus).astype(bf16)
    packed, plus_a, minus_b, plus_b, minus_a = tied(packed, plus_a, minus_b, plus_b, minus_a)
    plus_b, minus_a = send(plus_b, OUTER, 1), send(minus_a, OUTER, 3)
    plus_a, minus_b = send(plus_a, OUTER, 1), send(minus_b, OUTER, 3)
    got = lax.all_to_all(packed, "fsdp", split_axis=0, concat_axis=0, tiled=True)
    seed, moments = unpack(rows_taken, got)
    u = [add(stay_a[s], plus_a[s], minus_a[s]).astype(bf16) for s in range(2)]
    u += [add(stay_b[s], plus_b[s], minus_b[s]).astype(bf16) for s in range(2)]

    two = jnp.stack([seed, send(seed, PAIR)])
    own = jnp.stack([two] + [send(two, INNER, s) for s in (1, 2, 3)])

    own, *u = tied(own, *u)
    got = [send(u[s], INNER, s) for s in (2, 1, 3)]
    plus, minus = send(own, OUTER, 1), send(own, OUTER, 3)
    away = add(u[0][1], *[g[1] for g in got]).astype(bf16)
    away, plus, minus = tied(away, plus, minus)
    got_away = send(away, PAIR)
    far = (send(plus[:2], OUTER, 1), send(minus[2:], OUTER, 3))
    near = (own, plus, minus)
    near_other = tuple(send(p, CORE) for p in near)
    partial = add(u[0][0], *[g[0] for g in got], got_away).astype(bf16)

    partial, *near_other = tied(partial, *near_other)
    near_other = tuple(near_other)
    replica = send(partial, REPLICA)
    start, near_grads = near_products(place, tokens, key_grads, near + near_other)
    gradient = partial.astype(f32) + replica.astype(f32)
    *far, gradient, start = tied(*far, gradient, start)
    far = tuple(far)
    far_other = tuple(send(p, CORE) for p in far)
    gradient_other = send(gradient, CORE)
    keys, input_grads = far_products(
        place, tokens, key_grads, start, near_grads, near + far + near_other + far_other
    )

    moments_zh = send(moments, REPLICA)
    halves = jnp.concatenate(
        [
            ordered(zh, moments[:, :QUARTER], moments_zh[:, :QUARTER], 1),
            ordered(zh, moments[:, QUARTER:], moments_zh[:, QUARTER:], 1),
        ],
        axis=1,
    )
    halves_other = send(halves, CORE)
    seed_other = near_other[0][0, 0]

    new_param, new_first, new_second = adamw(
        place, (gradient, seed, halves), (gradient_other, seed_other, halves_other)
    )
    return (keys, input_grads, new_param, new_first, new_second)


def solution(mesh):
    over_all = P(("fsdp", "dp"), None)
    over_fsdp = P("fsdp", None)
    return jax.shard_map(
        on_device,
        mesh=mesh,
        in_specs=(over_all, over_all, over_fsdp, over_fsdp, over_fsdp, P()),
        out_specs=(over_all, over_all, over_fsdp, over_fsdp, over_fsdp),
        check_vma=False,
    )
```

time: 357 us -> 197 us (0.55)
  Pallas kernels: 186 us -> 45.8 us
  blocking collectives: 24.9 us -> 0 us
  starting transfers between devices: 64.2 us -> 45.3 us
  waiting for transfers between devices: 65.2 us -> 78.9 us
  local copies, waits for them, and re-layouts: 6.74 us -> 13.9 us
    pallas_call x3 -> x5, Pallas kernels: 181 us -> 39.2 us  [the longest x1 11.7 us: near_products(): pl.pallas_call(near_kernel, out_shape=(jax.ShapeDtypeStruct((TOK, C), f32...]
    ppermute x33 -> x28, starting transfers between devices: 64.2 us -> 38.2 us  [send(): return lax.ppermute(array, AXES, shift_pairs(axis_of_core, shift))]
    all_to_all x1 -> x0, blocking collectives: 24.9 us -> none  [on_device(): lax.all_to_all(packed, 'fsdp', split_axis=0, concat_axis=0, tiled=True)]
    all_to_all x0 -> x1, waiting for transfers between devices: none -> 9.68 us  [on_device(): lax.all_to_all(packed, 'fsdp', split_axis=0, concat_axis=0, tiled=True)]
    all_to_all x0 -> x1, starting transfers between devices: none -> 7.12 us  [on_device(): lax.all_to_all(packed, 'fsdp', split_axis=0, concat_axis=0, tiled=True)]
    unnamed x34 -> x46, local copies, waits for them, and re-layouts: 4.77 us -> 11.9 us
    convert_element_type x4 -> x5, other arithmetic: 2.89 us -> 8.85 us  [the longest x1 2.44 us: on_device(): plus_a = add(plus_a, far_plus).astype(bf16)]
    ppermute x33 -> x28, waiting for transfers between devices: 65.2 us -> 69.2 us  [send(): return lax.ppermute(array, AXES, shift_pairs(axis_of_core, shift))]
  transfers between devices with their start and end apart: 33 -> 29, of which waited for: 8 -> 14; matrix products, arithmetic and copies ran while one was open for 3% -> 5% of each run, Pallas kernels for 13% -> 11%
where the time goes in v2:
time: 197 us
  waiting for transfers between devices  78.9 us (40%)
  Pallas kernels  45.8 us (23%)
  starting transfers between devices  45.3 us (23%)
  local copies, waits for them, and re-layouts  13.9 us (7%)
  other arithmetic  11.4 us (6%)
    ppermute x28, waiting for transfers between devices, send(): return lax.ppermute(array, AXES, shift_pairs(axis_of_core, shift))  69.2 us
    ppermute x28, starting transfers between devices, send(): return lax.ppermute(array, AXES, shift_pairs(axis_of_core, shift))  38.2 us
    unnamed x46, local copies, waits for them, and re-layouts  11.9 us
    pallas_call x1, Pallas kernels, near_products(): pl.pallas_call(near_kernel, out_shape=(jax.ShapeDtypeStruct((TOK, C), f32...  11.7 us
    pallas_call x1, Pallas kernels, split_tokens(): pl.pallas_call(split_kernel, out_shape=(jax.ShapeDtypeStruct((TOK, D // 2...  10.2 us
    pallas_call x1, Pallas kernels, far_products(): pl.pallas_call(far_kernel, out_shape=(jax.ShapeDtypeStruct((TOK, C), bf16...  10 us
    all_to_all x1, waiting for transfers between devices, on_device(): lax.all_to_all(packed, 'fsdp', split_axis=0, concat_axis=0, tiled=True)  9.68 us
    all_to_all x1, starting transfers between devices, on_device(): lax.all_to_all(packed, 'fsdp', split_axis=0, concat_axis=0, tiled=True)  7.12 us
  transfers between devices with their start and end apart: 29, of which 14 were waited for; matrix products, arithmetic and copies ran while one was open for 5% of the time, Pallas kernels for 11%

profile of v2, /device:TPU:1, one launch (start us, length us, event | category | flops | bytes accessed | tf_op | source)
XLA Modules:
  0.0 196.5 jit_solution(8671298551204754518)
XLA Ops:
  1.4 10.2 %shard_map.102 = (bf16[256,8192]{1,0:T(8,128)(2,1)}, bf16[256,8704]{1,0:T(8,128)(2,1)}) custom-call(s32[5]{0:T(128)} %stack.56.place, bf16[256,16384]{1,0:T(8,128)(2,1)} %tokens.5, bf16[256,512]{1,0:T(8,128)(2,1)} %key_grads.7), custom_call_target="tpu_custom_call" | custom-call | bytes 1024 | tf_op jit(solution)/shard_map/pallas_call | solution.py:78
  13.0 7.4 %collective-permute-done.theirs = bf16[256,8704]{1,0:T(8,128)(2,1)S(1)} collective-permute-done((bf16[256,8704]{1,0:T(8,128)(2,1)}, bf16[256,8704]{1,0:T(8,128)(2,1)S(1)}, u32[]{:S(2)}, u32[]{:S(2)}) %collective-permute-start) | collective-permute-done | bytes 4456480 | tf_op jit(solution)/shard_map/ppermute | solution.py:56
  20.4 3.8 %copy-done.2 = bf16[256,8192]{1,0:T(8,128)(2,1)S(1)} copy-done((bf16[256,8192]{1,0:T(8,128)(2,1)S(1)}, bf16[256,8192]{1,0:T(8,128)(2,1)}, u32[]{:S(2)}) %copy-start.2) | copy-done | bytes 4194328
  24.2 3.2 %shard_map.103 = (bf16[2,2,512,256]{3,2,1,0:T(8,128)(2,1)}, bf16[2,2,512,256]{3,2,1,0:T(8,128)(2,1)}, bf16[512,512]{1,0:T(8,128)(2,1)S(1)}) custom-call(s32[5]{0:T(128)S(1)} %copy-done.10, bf16[256,8192]{1,0:T(8,128)(2,1)S(1)} %copy-done.2, bf16[256,8704]{1,0:T(8,128)(2,1)S(1)} %collective-permute-done.theirs, bf16[256,512]{1,0:T(8,128)(2,1)S(1)} %copy-done.4), custom_call_target="tpu_custom_call" | custom-call | bytes 1024 | tf_op jit(solution)/shard_map/pallas_call | solution.py:197
  33.9 2.0 shard_map.101
  36.6 2.2 %copy-done.3 = bf16[256,8192]{1,0:T(8,128)(2,1)S(1)} copy-done((bf16[256,8192]{1,0:T(8,128)(2,1)S(1)}, bf16[256,8192]{1,0:T(8,128)(2,1)}, u32[]{:S(2)}) %copy-start.3) | copy-done | bytes 4194328
  38.8 4.1 %shard_map.104 = (bf16[2,2,512,256]{3,2,1,0:T(8,128)(2,1)S(1)}, bf16[2,2,512,256]{3,2,1,0:T(8,128)(2,1)S(1)}, bf16[2,2,512,256]{3,2,1,0:T(8,128)(2,1)S(1)}, bf16...) custom-call(s32[5]{0:T(128)S(1)} %copy-done.10, ...), custom_call_target="tpu_custom_call" | custom-call | bytes 1024 | tf_op jit(solution)/shard_map/pallas_call | solution.py:205
  43.8 2.4 %add_convert_fusion.1 = bf16[2,2,512,256]{3,2,1,0:T(8,128)(2,1)} fusion(bf16[2,2,512,256]{3,2,1,0:T(8,128)(2,1)} %collective-permute-done.1, bf16[2,2,512,256]{3,2,1,0:T(8,128)(2,1)S(1)} %get-tuple-element.49), kind=kLoop, calls=%fused_computation.2 | loop fusion | flops 2097152 | bytes 3145728 | tf_op jit(solution)/shard_map/convert_element_type | solution.py:420
  46.2 2.4 %add_convert_fusion = bf16[2,2,512,256]{3,2,1,0:T(8,128)(2,1)} fusion(bf16[2,2,512,256]{3,2,1,0:T(8,128)(2,1)} %collective-permute-done.2, bf16[2,2,512,256]{3,2,1,0:T(8,128)(2,1)S(1)} %get-tuple-element.51), kind=kLoop, calls=%fused_computation.1 | loop fusion | flops 2097152 | bytes 3145728 | tf_op jit(solution)/shard_map/convert_element_type | solution.py:421
  48.7 7.1 %all-to-all-start = ((bf16[32,32,512]{2,1,0:T(8,128)(2,1)}), bf16[32,32,512]{2,1,0:T(8,128)(2,1)S(1)}, u32[]{:S(2)}, u32[]{:S(2)}) async-start(bf16[32,32,512]{2,1,0:T(8,128)(2,1)} %bitcast.7), calls=%async_computation | async-start | bytes 2097152 | tf_op jit(solution)/shard_map/all_to_all | solution.py:425
  55.8 2.5 %collective-permute-start.8 = (bf16[2,2,512,256]{3,2,1,0:T(8,128)(2,1)}, bf16[2,2,512,256]{3,2,1,0:T(8,128)(2,1)}, u32[]{:S(2)}, u32[]{:S(2)}) collective-permute-start(bf16[2,2,512,256]{3,2,1,0:T(8,128)(2,1)} %copy-done.13), channel_id=1, source_target_pairs={{0,12},{1,49},{2,14},{3,51},{64,76},{65,113},{66,78},{67,115},{16,... | collective-permute-start | bytes 3145736 | tf_op jit(solution)/shard_map/ppermute | solution.py:56
  58.3 2.7 %collective-permute-start.10 = (bf16[2,2,512,256]{3,2,1,0:T(8,128)(2,1)}, bf16[2,2,512,256]{3,2,1,0:T(8,128)(2,1)}, u32[]{:S(2)}, u32[]{:S(2)}) collective-permute-start(bf16[2,2,512,256]{3,2,1,0:T(8,128)(2,1)} %add_convert_fusion), channel_id=1, source_target_pairs={{0,12},{1,49},{2,14},{3,51},{64,76},{65,113},{66,78},{67,115},{16,... | collective-permute-start | bytes 3145736 | tf_op jit(solution)/shard_map/ppermute | solution.py:56
  61.0 9.7 %all-to-all-done = bf16[32,32,512]{2,1,0:T(8,128)(2,1)S(1)} async-done(((bf16[32,32,512]{2,1,0:T(8,128)(2,1)}), bf16[32,32,512]{2,1,0:T(8,128)(2,1)S(1)}, u32[]{:S(2)}, u32[]{:S(2)}) %all-to-all-start) | async-done | bytes 1048608 | tf_op jit(solution)/shard_map/all_to_all | solution.py:425
  72.7 5.0 %collective-permute-done.3 = bf16[512,256]{1,0:T(8,128)(2,1)S(1)} collective-permute-done((bf16[512,256]{1,0:T(8,128)(2,1)S(1)}, bf16[512,256]{1,0:T(8,128)(2,1)S(1)}, u32[]{:S(2)}, u32[]{:S(2)}) %collective-permute-start.3) | collective-permute-done | bytes 262176 | tf_op jit(solution)/shard_map/ppermute | solution.py:56
  78.6 2.3 %collective-permute-done.8 = bf16[2,2,512,256]{3,2,1,0:T(8,128)(2,1)} collective-permute-done((bf16[2,2,512,256]{3,2,1,0:T(8,128)(2,1)}, bf16[2,2,512,256]{3,2,1,0:T(8,128)(2,1)}, u32[]{:S(2)}, u32[]{:S(2)}) %collective-permute-start.8) | collective-permute-done | bytes 1048608 | tf_op jit(solution)/shard_map/ppermute | solution.py:56
  80.9 2.7 %collective-permute-start.5 = (bf16[2,512,256]{2,1,0:T(8,128)(2,1)S(1)}, bf16[2,512,256]{2,1,0:T(8,128)(2,1)S(1)}, u32[]{:S(2)}, u32[]{:S(2)}) collective-permute-start(bf16[2,512,256]{2,1,0:T(8,128)(2,1)S(1)} %get-tuple-element.99), channel_id=1, source_target_pairs={{0,32},{1,9},{2,34},{3,11},{64,96},{65,73},{66,98},{67,75},{16,48}... | collective-permute-start | bytes 1572872 | tf_op jit(solution)/shard_map/ppermute | solution.py:56
  85.8 13.7 %collective-permute-done.10 = bf16[2,2,512,256]{3,2,1,0:T(8,128)(2,1)} collective-permute-done((bf16[2,2,512,256]{3,2,1,0:T(8,128)(2,1)}, bf16[2,2,512,256]{3,2,1,0:T(8,128)(2,1)}, u32[]{:S(2)}, u32[]{:S(2)}) %collective-permute-start.10) | collective-permute-done | bytes 1048608 | tf_op jit(solution)/shard_map/ppermute | solution.py:56
  99.5 3.8 %collective-permute-done.9 = bf16[2,2,512,256]{3,2,1,0:T(8,128)(2,1)} collective-permute-done((bf16[2,2,512,256]{3,2,1,0:T(8,128)(2,1)}, bf16[2,2,512,256]{3,2,1,0:T(8,128)(2,1)}, u32[]{:S(2)}, u32[]{:S(2)}) %collective-permute-start.9) | collective-permute-done | bytes 1048608 | tf_op jit(solution)/shard_map/ppermute | solution.py:56
  103.3 1.9 fusion.3
  105.7 2.7 %collective-permute-start.15 = (bf16[4,2,512,256]{3,2,1,0:T(8,128)(2,1)S(1)}, bf16[4,2,512,256]{3,2,1,0:T(8,128)(2,1)S(1)}, u32[]{:S(2)}, u32[]{:S(2)}) collective-permute-start(bf16[4,2,512,256]{3,2,1,0:T(8,128)(2,1)S(1)} %pad_maximum_fusion.refs_0_), channel_id=1, source_target_pairs={{0,12},{1,49},{2,14},{3,51},{64,76},{65,113},{66,78},{67,115},{16,... | collective-permute-start | bytes 6291464 | tf_op jit(solution)/shard_map/ppermute | solution.py:56
  108.4 3.1 %collective-permute-start.13 = (bf16[2,512,256]{2,1,0:T(8,128)(2,1)S(1)}, bf16[2,512,256]{2,1,0:T(8,128)(2,1)S(1)}, u32[]{:S(2)}, u32[]{:S(2)}) collective-permute-start(bf16[2,512,256]{2,1,0:T(8,128)(2,1)S(1)} %get-tuple-element.66), channel_id=1, source_target_pairs={{0,48},{1,13},{2,50},{3,15},{64,112},{65,77},{66,114},{67,79},{16,... | collective-permute-start | bytes 1572872 | tf_op jit(solution)/shard_map/ppermute | solution.py:56
  112.7 11.9 %collective-permute-done.13 = bf16[2,512,256]{2,1,0:T(8,128)(2,1)S(1)} collective-permute-done((bf16[2,512,256]{2,1,0:T(8,128)(2,1)S(1)}, bf16[2,512,256]{2,1,0:T(8,128)(2,1)S(1)}, u32[]{:S(2)}, u32[]{:S(2)}) %collective-permute-start.13) | collective-permute-done | bytes 524320 | tf_op jit(solution)/shard_map/ppermute | solution.py:56
  128.2 8.3 %collective-permute-done.11 = bf16[2,512,256]{2,1,0:T(8,128)(2,1)S(1)} collective-permute-done((bf16[2,512,256]{2,1,0:T(8,128)(2,1)S(1)}, bf16[2,512,256]{2,1,0:T(8,128)(2,1)S(1)}, u32[]{:S(2)}, u32[]{:S(2)}) %collective-permute-start.11) | collective-permute-done | bytes 524320 | tf_op jit(solution)/shard_map/ppermute | solution.py:56
  136.6 6.7 %collective-permute-done.14.refs_1_ = bf16[4,2,512,256]{3,2,1,0:T(8,128)(2,1)S(1)} collective-permute-done((bf16[4,2,512,256]{3,2,1,0:T(8,128)(2,1)S(1)}, bf16[4,2,512,256]{3,2,1,0:T(8,128)(2,1)S(1)}, u32[]{:S(2)}, u32[]{:S(2)}) %collective-permute-start.14) | collective-permute-done | bytes 2097184 | tf_op jit(solution)/shard_map/ppermute | solution.py:56
  143.4 2.7 %collective-permute-start.20 = (bf16[4,2,512,256]{3,2,1,0:T(8,128)(2,1)S(1)}, bf16[4,2,512,256]{3,2,1,0:T(8,128)(2,1)S(1)}, u32[]{:S(2)}, u32[]{:S(2)}) collective-permute-start(bf16[4,2,512,256]{3,2,1,0:T(8,128)(2,1)S(1)} %collective-permute-done.14.refs_1_), channel_id=1, source_target_pairs={{0,1},{1,0},{2,3},{3,2},{64,65},{65,64},{66,67},{67,66},{16,17},{1... | collective-permute-start | bytes 6291464 | tf_op jit(solution)/shard_map/ppermute | solution.py:56
  148.8 4.9 %collective-permute-done.18 = bf16[512,256]{1,0:T(8,128)(2,1)S(1)} collective-permute-done((bf16[512,256]{1,0:T(8,128)(2,1)S(1)}, bf16[512,256]{1,0:T(8,128)(2,1)S(1)}, u32[]{:S(2)}, u32[]{:S(2)}) %collective-permute-start.18) | collective-permute-done | bytes 262176 | tf_op jit(solution)/shard_map/ppermute | solution.py:56
  153.7 2.4 %collective-permute-start.17 = (bf16[2,2,512,256]{3,2,1,0:T(8,128)(2,1)S(1)}, bf16[2,2,512,256]{3,2,1,0:T(8,128)(2,1)}, u32[]{:S(2)}, u32[]{:S(2)}) collective-permute-start(bf16[2,2,512,256]{3,2,1,0:T(8,128)(2,1)S(1)} %slice.98), channel_id=1, source_target_pairs={{0,12},{1,49},{2,14},{3,51},{64,76},{65,113},{66,78},{67,115},{16,... | collective-permute-start | bytes 3145736 | tf_op jit(solution)/shard_map/ppermute | solution.py:56
  157.7 3.3 %collective-permute-start.22 = (bf16[512,256]{1,0:T(8,128)(2,1)S(1)}, bf16[512,256]{1,0:T(8,128)(2,1)S(1)}, u32[]{:S(2)}, u32[]{:S(2)}) collective-permute-start(bf16[512,256]{1,0:T(8,128)(2,1)S(1)} %fusion.4), channel_id=1, source_target_pairs={{0,2},{1,3},{2,0},{3,1},{64,66},{65,67},{66,64},{67,65},{16,18},{1... | collective-permute-start | bytes 786440 | tf_op jit(solution)/shard_map/ppermute | solution.py:56
  162.4 11.7 %shard_map.106 = (f32[256,512]{1,0:T(8,128)}, bf16[256,16384]{1,0:T(8,128)(2,1)}) custom-call(s32[5]{0:T(128)} %stack.56.place, bf16[256,16384]{1,0:T(8,128)(2,1)} %tokens.5, bf16[256,512]{1,0:T(8,128)(2,1)} %key_grads.7, bf16[4,2,512,256]{3,2,1,0:T(8,128)(2,1)} %copy-done.14, bf16[4,2,512,256]{3,2,1,0:T(8,128)(2,1)} %copy-done.15, ...), custom_call_target="tpu_custom_call" | custom-call | bytes 1024 | tf_op jit(solution)/shard_map/pallas_call | solution.py:303
  174.3 2.2 %collective-permute-start.23 = (bf16[2,2,512,256]{3,2,1,0:T(8,128)(2,1)}, bf16[2,2,512,256]{3,2,1,0:T(8,128)(2,1)S(1)}, u32[]{:S(2)}, u32[]{:S(2)}) collective-permute-start(bf16[2,2,512,256]{3,2,1,0:T(8,128)(2,1)} %collective-permute-done.16.refs_3_), channel_id=1, source_target_pairs={{0,1},{1,0},{2,3},{3,2},{64,65},{65,64},{66,67},{67,66},{16,17},{1... | collective-permute-start | bytes 3145736 | tf_op jit(solution)/shard_map/ppermute | solution.py:56
  181.7 3.3 %shard_map.108 = (bf16[512,512]{1,0:T(8,128)(2,1)}, f32[512,512]{1,0:T(8,128)}, f32[512,512]{1,0:T(8,128)}) custom-call(s32[5]{0:T(128)S(1)} %copy-done.11, f32[512,256]{1,0:T(8,128)S(1)} %convert_add_fusion.grads, bf16[512,256]{1,0:T(8,128)(2,1)S(1)} %get-tuple-element.56.weights, bf16[512,512]{1,0:T(8,128)(2,1)S(1)} %pad_maximum_fusion.2.moments, ...), custom_call_target="tpu_custom_call" | custom-call | bytes 1024 | tf_op jit(solution)/shard_map/pallas_call | solution.py:390
  186.3 10.0 %shard_map.107 = (bf16[256,512]{1,0:T(8,128)(2,1)}, bf16[256,16384]{1,0:T(8,128)(2,1)}) custom-call(s32[5]{0:T(128)} %stack.56.place, bf16[256,16384]{1,0:T(8,128)(2,1)} %tokens.5, bf16[256,512]{1,0:T(8,128)(2,1)} %key_grads.7, f32[256,512]{1,0:T(8,128)} %get-tuple-element.76.start, ...), custom_call_target="tpu_custom_call", output_to_operand_aliasing={{1}: (4, {})} | custom-call | bytes 1024 | tf_op jit(solution)/shard_map/pallas_call | solution.py:318
  (104 shorter events, 33.1 us)
Async XLA Ops:
  1.4 19.0 %copy-start.10 = (s32[5]{0:T(128)S(1)}, s32[5]{0:T(128)}, u32[]{:S(2)}) copy-start(s32[5]{0:T(128)} %stack.56.place) | copy-start | bytes 64
  11.6 8.8 %collective-permute-start = (bf16[256,8704]{1,0:T(8,128)(2,1)}, bf16[256,8704]{1,0:T(8,128)(2,1)S(1)}, u32[]{:S(2)}, u32[]{:S(2)}) collective-permute-start(bf16[256,8704]{1,0:T(8,128)(2,1)} %get-tuple-element.47), channel_id=1, source_target_pairs={{0,1},{1,0},{2,3},{3,2},{64,65},{65,64},{66,67},{67,66},{16,17},{1... | collective-permute-start | bytes 13369352 | tf_op jit(solution)/shard_map/ppermute | solution.py:56
  28.2 15.6 %collective-permute-start.1 = (bf16[2,2,512,256]{3,2,1,0:T(8,128)(2,1)}, bf16[2,2,512,256]{3,2,1,0:T(8,128)(2,1)}, u32[]{:S(2)}, u32[]{:S(2)}) collective-permute-start(bf16[2,2,512,256]{3,2,1,0:T(8,128)(2,1)} %get-tuple-element.50), channel_id=1, source_target_pairs={{0,4},{1,17},{2,6},{3,19},{64,68},{65,81},{66,70},{67,83},{16,20},... | collective-permute-start | bytes 3145736 | tf_op jit(solution)/shard_map/ppermute | solution.py:56
  29.5 16.7 %collective-permute-start.2 = (bf16[2,2,512,256]{3,2,1,0:T(8,128)(2,1)}, bf16[2,2,512,256]{3,2,1,0:T(8,128)(2,1)}, u32[]{:S(2)}, u32[]{:S(2)}) collective-permute-start(bf16[2,2,512,256]{3,2,1,0:T(8,128)(2,1)} %get-tuple-element.52), channel_id=1, source_target_pairs={{0,12},{1,49},{2,14},{3,51},{64,76},{65,113},{66,78},{67,115},{16,... | collective-permute-start | bytes 3145736 | tf_op jit(solution)/shard_map/ppermute | solution.py:56
  48.7 22.0 %all-to-all-start = ((bf16[32,32,512]{2,1,0:T(8,128)(2,1)}), bf16[32,32,512]{2,1,0:T(8,128)(2,1)S(1)}, u32[]{:S(2)}, u32[]{:S(2)}) async-start(bf16[32,32,512]{2,1,0:T(8,128)(2,1)} %bitcast.7), calls=%async_computation | async-start | bytes 2097152 | tf_op jit(solution)/shard_map/all_to_all | solution.py:425
  55.8 25.1 %collective-permute-start.8 = (bf16[2,2,512,256]{3,2,1,0:T(8,128)(2,1)}, bf16[2,2,512,256]{3,2,1,0:T(8,128)(2,1)}, u32[]{:S(2)}, u32[]{:S(2)}) collective-permute-start(bf16[2,2,512,256]{3,2,1,0:T(8,128)(2,1)} %copy-done.13), channel_id=1, source_target_pairs={{0,12},{1,49},{2,14},{3,51},{64,76},{65,113},{66,78},{67,115},{16,... | collective-permute-start | bytes 3145736 | tf_op jit(solution)/shard_map/ppermute | solution.py:56
  58.3 25.3 %collective-permute-start.7 = (bf16[2,2,512,256]{3,2,1,0:T(8,128)(2,1)}, bf16[2,2,512,256]{3,2,1,0:T(8,128)(2,1)}, u32[]{:S(2)}, u32[]{:S(2)}) collective-permute-start(bf16[2,2,512,256]{3,2,1,0:T(8,128)(2,1)} %add_convert_fusion.1), channel_id=1, source_target_pairs={{0,4},{1,17},{2,6},{3,19},{64,68},{65,81},{66,70},{67,83},{16,20},... | collective-permute-start | bytes 3145736 | tf_op jit(solution)/shard_map/ppermute | solution.py:56
  58.3 41.2 %collective-permute-start.10 = (bf16[2,2,512,256]{3,2,1,0:T(8,128)(2,1)}, bf16[2,2,512,256]{3,2,1,0:T(8,128)(2,1)}, u32[]{:S(2)}, u32[]{:S(2)}) collective-permute-start(bf16[2,2,512,256]{3,2,1,0:T(8,128)(2,1)} %add_convert_fusion), channel_id=1, source_target_pairs={{0,12},{1,49},{2,14},{3,51},{64,76},{65,113},{66,78},{67,115},{16,... | collective-permute-start | bytes 3145736 | tf_op jit(solution)/shard_map/ppermute | solution.py:56
  61.0 42.3 %collective-permute-start.9 = (bf16[2,2,512,256]{3,2,1,0:T(8,128)(2,1)}, bf16[2,2,512,256]{3,2,1,0:T(8,128)(2,1)}, u32[]{:S(2)}, u32[]{:S(2)}) collective-permute-start(bf16[2,2,512,256]{3,2,1,0:T(8,128)(2,1)} %copy-done.12), channel_id=1, source_target_pairs={{0,4},{1,17},{2,6},{3,19},{64,68},{65,81},{66,70},{67,83},{16,20},... | collective-permute-start | bytes 3145736 | tf_op jit(solution)/shard_map/ppermute | solution.py:56
  72.0 5.6 %collective-permute-start.3 = (bf16[512,256]{1,0:T(8,128)(2,1)S(1)}, bf16[512,256]{1,0:T(8,128)(2,1)S(1)}, u32[]{:S(2)}, u32[]{:S(2)}) collective-permute-start(bf16[512,256]{1,0:T(8,128)(2,1)S(1)} %get-tuple-element.56.weights), channel_id=1, source_target_pairs={{0,64},{1,65},{2,66},{3,67},{64,0},{65,1},{66,2},{67,3},{16,80},{1... | collective-permute-start | bytes 786440 | tf_op jit(solution)/shard_map/ppermute | solution.py:56
  77.7 27.4 %collective-permute-start.6 = (bf16[2,512,256]{2,1,0:T(8,128)(2,1)S(1)}, bf16[2,512,256]{2,1,0:T(8,128)(2,1)S(1)}, u32[]{:S(2)}, u32[]{:S(2)}) collective-permute-start(bf16[2,512,256]{2,1,0:T(8,128)(2,1)S(1)} %get-tuple-element.99), channel_id=1, source_target_pairs={{0,48},{1,13},{2,50},{3,15},{64,112},{65,77},{66,114},{67,79},{16,... | collective-permute-start | bytes 1572872 | tf_op jit(solution)/shard_map/ppermute | solution.py:56
  80.9 24.2 %collective-permute-start.5 = (bf16[2,512,256]{2,1,0:T(8,128)(2,1)S(1)}, bf16[2,512,256]{2,1,0:T(8,128)(2,1)S(1)}, u32[]{:S(2)}, u32[]{:S(2)}) collective-permute-start(bf16[2,512,256]{2,1,0:T(8,128)(2,1)S(1)} %get-tuple-element.99), channel_id=1, source_target_pairs={{0,32},{1,9},{2,34},{3,11},{64,96},{65,73},{66,98},{67,75},{16,48}... | collective-permute-start | bytes 1572872 | tf_op jit(solution)/shard_map/ppermute | solution.py:56
  83.6 21.6 %collective-permute-start.4 = (bf16[2,512,256]{2,1,0:T(8,128)(2,1)S(1)}, bf16[2,512,256]{2,1,0:T(8,128)(2,1)S(1)}, u32[]{:S(2)}, u32[]{:S(2)}) collective-permute-start(bf16[2,512,256]{2,1,0:T(8,128)(2,1)S(1)} %get-tuple-element.99), channel_id=1, source_target_pairs={{0,16},{1,5},{2,18},{3,7},{64,80},{65,69},{66,82},{67,71},{16,32},... | collective-permute-start | bytes 1572872 | tf_op jit(solution)/shard_map/ppermute | solution.py:56
  105.5 42.0 %copy-start.14 = (bf16[4,2,512,256]{3,2,1,0:T(8,128)(2,1)}, bf16[4,2,512,256]{3,2,1,0:T(8,128)(2,1)S(1)}, u32[]{:S(2)}) copy-start(bf16[4,2,512,256]{3,2,1,0:T(8,128)(2,1)S(1)} %pad_maximum_fusion.refs_0_) | copy-start | bytes 6291460
  105.5 37.9 %collective-permute-start.14 = (bf16[4,2,512,256]{3,2,1,0:T(8,128)(2,1)S(1)}, bf16[4,2,512,256]{3,2,1,0:T(8,128)(2,1)S(1)}, u32[]{:S(2)}, u32[]{:S(2)}) collective-permute-start(bf16[4,2,512,256]{3,2,1,0:T(8,128)(2,1)S(1)} %pad_maximum_fusion.refs_0_), channel_id=1, source_target_pairs={{0,4},{1,17},{2,6},{3,19},{64,68},{65,81},{66,70},{67,83},{16,20},... | collective-permute-start | bytes 6291464 | tf_op jit(solution)/shard_map/ppermute | solution.py:56
  105.7 37.6 %collective-permute-start.15 = (bf16[4,2,512,256]{3,2,1,0:T(8,128)(2,1)S(1)}, bf16[4,2,512,256]{3,2,1,0:T(8,128)(2,1)S(1)}, u32[]{:S(2)}, u32[]{:S(2)}) collective-permute-start(bf16[4,2,512,256]{3,2,1,0:T(8,128)(2,1)S(1)} %pad_maximum_fusion.refs_0_), channel_id=1, source_target_pairs={{0,12},{1,49},{2,14},{3,51},{64,76},{65,113},{66,78},{67,115},{16,... | collective-permute-start | bytes 6291464 | tf_op jit(solution)/shard_map/ppermute | solution.py:56
  108.4 16.2 %collective-permute-start.13 = (bf16[2,512,256]{2,1,0:T(8,128)(2,1)S(1)}, bf16[2,512,256]{2,1,0:T(8,128)(2,1)S(1)}, u32[]{:S(2)}, u32[]{:S(2)}) collective-permute-start(bf16[2,512,256]{2,1,0:T(8,128)(2,1)S(1)} %get-tuple-element.66), channel_id=1, source_target_pairs={{0,48},{1,13},{2,50},{3,15},{64,112},{65,77},{66,114},{67,79},{16,... | collective-permute-start | bytes 1572872 | tf_op jit(solution)/shard_map/ppermute | solution.py:56
  111.5 16.7 %collective-permute-start.12 = (bf16[2,512,256]{2,1,0:T(8,128)(2,1)S(1)}, bf16[2,512,256]{2,1,0:T(8,128)(2,1)S(1)}, u32[]{:S(2)}, u32[]{:S(2)}) collective-permute-start(bf16[2,512,256]{2,1,0:T(8,128)(2,1)S(1)} %get-tuple-element.65), channel_id=1, source_target_pairs={{0,16},{1,5},{2,18},{3,7},{64,80},{65,69},{66,82},{67,71},{16,32},... | collective-permute-start | bytes 1572872 | tf_op jit(solution)/shard_map/ppermute | solution.py:56
  111.5 25.0 %collective-permute-start.11 = (bf16[2,512,256]{2,1,0:T(8,128)(2,1)S(1)}, bf16[2,512,256]{2,1,0:T(8,128)(2,1)S(1)}, u32[]{:S(2)}, u32[]{:S(2)}) collective-permute-start(bf16[2,512,256]{2,1,0:T(8,128)(2,1)S(1)} %get-tuple-element.64), channel_id=1, source_target_pairs={{0,32},{1,9},{2,34},{3,11},{64,96},{65,73},{66,98},{67,75},{16,48}... | collective-permute-start | bytes 1572872 | tf_op jit(solution)/shard_map/ppermute | solution.py:56
  124.6 31.7 %collective-permute-start.19 = (bf16[4,2,512,256]{3,2,1,0:T(8,128)(2,1)S(1)}, bf16[4,2,512,256]{3,2,1,0:T(8,128)(2,1)S(1)}, u32[]{:S(2)}, u32[]{:S(2)}) collective-permute-start(bf16[4,2,512,256]{3,2,1,0:T(8,128)(2,1)S(1)} %pad_maximum_fusion.refs_0_), channel_id=1, source_target_pairs={{0,1},{1,0},{2,3},{3,2},{64,65},{65,64},{66,67},{67,66},{16,17},{1... | collective-permute-start | bytes 6291464 | tf_op jit(solution)/shard_map/ppermute | solution.py:56
  143.4 19.1 %copy-start.16 = (bf16[4,2,512,256]{3,2,1,0:T(8,128)(2,1)}, bf16[4,2,512,256]{3,2,1,0:T(8,128)(2,1)S(1)}, u32[]{:S(2)}) copy-start(bf16[4,2,512,256]{3,2,1,0:T(8,128)(2,1)S(1)} %collective-permute-done.15.refs_2_) | copy-start | bytes 6291460
  143.4 13.0 %collective-permute-start.20 = (bf16[4,2,512,256]{3,2,1,0:T(8,128)(2,1)S(1)}, bf16[4,2,512,256]{3,2,1,0:T(8,128)(2,1)S(1)}, u32[]{:S(2)}, u32[]{:S(2)}) collective-permute-start(bf16[4,2,512,256]{3,2,1,0:T(8,128)(2,1)S(1)} %collective-permute-done.14.refs_1_), channel_id=1, source_target_pairs={{0,1},{1,0},{2,3},{3,2},{64,65},{65,64},{66,67},{67,66},{16,17},{1... | collective-permute-start | bytes 6291464 | tf_op jit(solution)/shard_map/ppermute | solution.py:56
  146.0 10.3 %collective-permute-start.21 = (bf16[4,2,512,256]{3,2,1,0:T(8,128)(2,1)S(1)}, bf16[4,2,512,256]{3,2,1,0:T(8,128)(2,1)S(1)}, u32[]{:S(2)}, u32[]{:S(2)}) collective-permute-start(bf16[4,2,512,256]{3,2,1,0:T(8,128)(2,1)S(1)} %collective-permute-done.15.refs_2_), channel_id=1, source_target_pairs={{0,1},{1,0},{2,3},{3,2},{64,65},{65,64},{66,67},{67,66},{16,17},{1... | collective-permute-start | bytes 6291464 | tf_op jit(solution)/shard_map/ppermute | solution.py:56
  146.1 7.6 %collective-permute-start.18 = (bf16[512,256]{1,0:T(8,128)(2,1)S(1)}, bf16[512,256]{1,0:T(8,128)(2,1)S(1)}, u32[]{:S(2)}, u32[]{:S(2)}) collective-permute-start(bf16[512,256]{1,0:T(8,128)(2,1)S(1)} %fusion.5), channel_id=1, source_target_pairs={{0,64},{1,65},{2,66},{3,67},{64,0},{65,1},{66,2},{67,3},{16,80},{1... | collective-permute-start | bytes 786440 | tf_op jit(solution)/shard_map/ppermute | solution.py:56
  147.5 26.8 %collective-permute-start.16 = (bf16[2,2,512,256]{3,2,1,0:T(8,128)(2,1)S(1)}, bf16[2,2,512,256]{3,2,1,0:T(8,128)(2,1)}, u32[]{:S(2)}, u32[]{:S(2)}) collective-permute-start(bf16[2,2,512,256]{3,2,1,0:T(8,128)(2,1)S(1)} %slice.97), channel_id=1, source_target_pairs={{0,4},{1,17},{2,6},{3,19},{64,68},{65,81},{66,70},{67,83},{16,20},... | collective-permute-start | bytes 3145736 | tf_op jit(solution)/shard_map/ppermute | solution.py:56
  153.7 20.6 %collective-permute-start.17 = (bf16[2,2,512,256]{3,2,1,0:T(8,128)(2,1)S(1)}, bf16[2,2,512,256]{3,2,1,0:T(8,128)(2,1)}, u32[]{:S(2)}, u32[]{:S(2)}) collective-permute-start(bf16[2,2,512,256]{3,2,1,0:T(8,128)(2,1)S(1)} %slice.98), channel_id=1, source_target_pairs={{0,12},{1,49},{2,14},{3,51},{64,76},{65,113},{66,78},{67,115},{16,... | collective-permute-start | bytes 3145736 | tf_op jit(solution)/shard_map/ppermute | solution.py:56
  157.7 16.5 %collective-permute-start.22 = (bf16[512,256]{1,0:T(8,128)(2,1)S(1)}, bf16[512,256]{1,0:T(8,128)(2,1)S(1)}, u32[]{:S(2)}, u32[]{:S(2)}) collective-permute-start(bf16[512,256]{1,0:T(8,128)(2,1)S(1)} %fusion.4), channel_id=1, source_target_pairs={{0,2},{1,3},{2,0},{3,1},{64,66},{65,67},{66,64},{67,65},{16,18},{1... | collective-permute-start | bytes 786440 | tf_op jit(solution)/shard_map/ppermute | solution.py:56
  161.0 15.5 %collective-permute-start.25 = (bf16[512,256]{1,0:T(8,128)(2,1)}, bf16[512,256]{1,0:T(8,128)(2,1)S(1)}, u32[]{:S(2)}, u32[]{:S(2)}) collective-permute-start(bf16[512,256]{1,0:T(8,128)(2,1)} %get-tuple-element.83), channel_id=1, source_target_pairs={{0,2},{1,3},{2,0},{3,1},{64,66},{65,67},{66,64},{67,65},{16,18},{1... | collective-permute-start | bytes 786440 | tf_op jit(solution)/shard_map/ppermute | solution.py:56
  174.3 10.8 %collective-permute-start.23 = (bf16[2,2,512,256]{3,2,1,0:T(8,128)(2,1)}, bf16[2,2,512,256]{3,2,1,0:T(8,128)(2,1)S(1)}, u32[]{:S(2)}, u32[]{:S(2)}) collective-permute-start(bf16[2,2,512,256]{3,2,1,0:T(8,128)(2,1)} %collective-permute-done.16.refs_3_), channel_id=1, source_target_pairs={{0,1},{1,0},{2,3},{3,2},{64,65},{65,64},{66,67},{67,66},{16,17},{1... | collective-permute-start | bytes 3145736 | tf_op jit(solution)/shard_map/ppermute | solution.py:56
  176.4 8.6 %collective-permute-start.24 = (bf16[2,2,512,256]{3,2,1,0:T(8,128)(2,1)}, bf16[2,2,512,256]{3,2,1,0:T(8,128)(2,1)S(1)}, u32[]{:S(2)}, u32[]{:S(2)}) collective-permute-start(bf16[2,2,512,256]{3,2,1,0:T(8,128)(2,1)} %collective-permute-done.17.refs_4_), channel_id=1, source_target_pairs={{0,1},{1,0},{2,3},{3,2},{64,65},{65,64},{66,67},{67,66},{16,17},{1... | collective-permute-start | bytes 3145736 | tf_op jit(solution)/shard_map/ppermute | solution.py:56
  177.6 3.4 %collective-permute-start.27 = (bf16[512,512]{1,0:T(8,128)(2,1)S(1)}, bf16[512,512]{1,0:T(8,128)(2,1)S(1)}, u32[]{:S(2)}, u32[]{:S(2)}) collective-permute-start(bf16[512,512]{1,0:T(8,128)(2,1)S(1)} %pad_maximum_fusion.2.moments), channel_id=1, source_target_pairs={{0,1},{1,0},{2,3},{3,2},{64,65},{65,64},{66,67},{67,66},{16,17},{1... | collective-permute-start | bytes 1572872 | tf_op jit(solution)/shard_map/ppermute | solution.py:56
  178.1 3.6 %collective-permute-start.26 = (f32[512,256]{1,0:T(8,128)S(1)}, f32[512,256]{1,0:T(8,128)S(1)}, u32[]{:S(2)}, u32[]{:S(2)}) collective-permute-start(f32[512,256]{1,0:T(8,128)S(1)} %convert_add_fusion.grads), channel_id=1, source_target_pairs={{0,1},{1,0},{2,3},{3,2},{64,65},{65,64},{66,67},{67,66},{16,17},{1... | collective-permute-start | bytes 1572872 | tf_op jit(solution)/shard_map/ppermute | solution.py:56
  (20 other events, 97.7 us)

commit v3 on v2

--- a/solution.py
+++ b/solution.py
@@ -63,31 +63,21 @@
 CORE = "cc"
 
 
-def split_kernel(place, tokens, key_grads, mine, out):
+def split_kernel(place, tokens, key_grads, out):
     core = place[3]
     for i in range(NF):
-        at = lambda k: pl.ds(pl.multiple_of(i * C + k * HALF, HALF), HALF)
-        mine[:, i * HALF : (i + 1) * HALF] = tokens[:, at(core)]
-        out[:, i * HALF : (i + 1) * HALF] = tokens[:, at(1 - core)]
+        at = pl.multiple_of(i * C + (1 - core) * HALF, HALF)
+        out[:, i * HALF : (i + 1) * HALF] = tokens[:, pl.ds(at, HALF)]
     out[:, D // 2 :] = key_grads[...]
 
 
 def split_tokens(place, tokens, key_grads):
-    rows = 32
-    band = lambda width: pl.BlockSpec((rows, width), lambda i, place: (i, 0))
     return pl.pallas_call(
         split_kernel,
-        out_shape=(
-            jax.ShapeDtypeStruct((TOK, D // 2), bf16),
-            jax.ShapeDtypeStruct((TOK, D // 2 + C), bf16),
-        ),
-        grid_spec=pltpu.PrefetchScalarGridSpec(
-            num_scalar_prefetch=1,
-            grid=(TOK // rows,),
-            in_specs=[band(D), band(C)],
-            out_specs=(band(D // 2), band(D // 2 + C)),
-        ),
-        compiler_params=pltpu.CompilerParams(vmem_limit_bytes=54 * 2**20),
+        out_shape=jax.ShapeDtypeStruct((TOK, D // 2 + C), bf16),
+        in_specs=[SMEM, VMEM, VMEM],
+        out_specs=VMEM,
+        compiler_params=pltpu.CompilerParams(vmem_limit_bytes=40 * 2**20),
         cost_estimate=LIGHT,
     )(place, tokens, key_grads)
 
@@ -158,59 +148,51 @@
     return (to_z * 4 + to_y) * 4 + to_x
 
 
-def gradient_term(place, mine, theirs, grads_t, outer, inner, pair):
+def gradient_term(place, tokens, theirs, grads_t, outer, inner, pair):
     core = place[3]
     f = target_index(place, core, outer, pair, inner, 1)
-    at = pl.ds(pl.multiple_of(f * HALF, HALF), HALF)
+    mine = tokens[:, pl.ds(pl.multiple_of(f * C + core * HALF, HALF), HALF)]
+    other = theirs[:, pl.ds(pl.multiple_of(f * HALF, HALF), HALF)]
     return jnp.dot(
-        grads_t[...],
-        jnp.concatenate([mine[:, at], theirs[:, at]], axis=0),
-        preferred_element_type=f32,
-    ).astype(bf16)
-
-
-def far_gradient_kernel(place, mine, theirs, key_grads, plus, minus, grads_t):
+        grads_t[...], jnp.concatenate([mine, other], axis=0), preferred_element_type=f32
+    )
+
+
+def first_gradient_kernel(place, tokens, theirs, key_grads, *refs):
+    outs, grads_t = refs[:6], refs[6]
     grads_t[:, :TOK] = key_grads[...].T
     grads_t[:, TOK:] = theirs[:, D // 2 :].T
-    for inner in range(2):
-        for pair in range(2):
-            term = functools.partial(gradient_term, place, mine, theirs, grads_t, 2)
-            plus[inner, pair] = term(inner, pair)
-            minus[inner, pair] = term(inner + 2, pair)
-
-
-def near_gradient_kernel(place, mine, theirs, grads_t, *refs):
-    for ref, (outer, first) in zip(refs, ((1, 2), (3, 0), (1, 0), (3, 2), (0, 0), (0, 2))):
+    halves = ((2, 0), (2, 2), (1, 2), (3, 0), (0, 0), (0, 2))
+    for ref, (outer, first) in zip(outs, halves):
 
         def body(inner, carry, ref=ref, outer=outer, first=first):
             for pair in range(2):
                 ref[inner, pair] = gradient_term(
-                    place, mine, theirs, grads_t, outer, first + inner, pair
-                )
+                    place, tokens, theirs, grads_t, outer, first + inner, pair
+                ).astype(bf16)
             return carry
 
         lax.fori_loop(0, 2, body, 0, unroll=2)
 
 
-def gradient_terms(place, mine, theirs, key_grads):
+def joined_gradient_kernel(place, tokens, theirs, grads_t, far_plus, far_minus, plus, minus):
+    for ref, far, outer, first in ((plus, far_plus, 1, 0), (minus, far_minus, 3, 2)):
+        for inner in range(2):
+            for pair in range(2):
+                term = gradient_term(place, tokens, theirs, grads_t, outer, first + inner, pair)
+                ref[inner, pair] = (term + far[inner, pair].astype(f32)).astype(bf16)
+
+
+def gradient_call(kernel, halves, others, cost, *args):
     half = jax.ShapeDtypeStruct((2, 2, C, HALF), bf16)
-    far_plus, far_minus, grads_t = pl.pallas_call(
-        far_gradient_kernel,
-        out_shape=(half, half, jax.ShapeDtypeStruct((C, 2 * TOK), bf16)),
-        in_specs=[SMEM, VMEM, VMEM, VMEM],
-        out_specs=(VMEM,) * 3,
-        compiler_params=pltpu.CompilerParams(vmem_limit_bytes=20 * 2**20),
-        cost_estimate=LIGHT,
-    )(place, mine, theirs, key_grads)
-    near = pl.pallas_call(
-        near_gradient_kernel,
-        out_shape=(half,) * 6,
-        in_specs=[SMEM, VMEM, VMEM, VMEM],
-        out_specs=(VMEM,) * 6,
+    return pl.pallas_call(
+        kernel,
+        out_shape=(half,) * halves + others,
+        in_specs=[SMEM] + [VMEM] * (len(args) - 1),
+        out_specs=(VMEM,) * (halves + len(others)),
         compiler_params=pltpu.CompilerParams(vmem_limit_bytes=24 * 2**20),
-        cost_estimate=LIGHT,
-    )(place, mine, theirs, grads_t)
-    return (far_plus, far_minus) + tuple(near)
+        cost_estimate=cost,
+    )(*args)
 
 
 def is_near(outer, inner):
@@ -409,25 +391,32 @@
     core, zh = d % 2, d // 2
     place = jnp.stack([f % 4, (f // 4) % 4, f // 16, core, zh])
 
-    mine, for_other = split_tokens(place, tokens, key_grads)
-    terms = gradient_terms(place, mine, send(for_other, CORE), key_grads)
-    far_plus, far_minus, plus_b, minus_a, plus_a, minus_b, stay_a, stay_b = terms
-
+    theirs = send(split_tokens(place, tokens, key_grads), CORE)
     table, rows_taken = routes(old_home, f, old_param.shape[0] // BR)
     packed = pack(place, table, old_param, old_first, old_second)
-
+    theirs, packed = tied(theirs, packed)
+
+    turned = (jax.ShapeDtypeStruct((C, 2 * TOK), bf16),)
+    far_plus, far_minus, plus_b, minus_a, stay_a, stay_b, grads_t = gradient_call(
+        first_gradient_kernel, 6, turned, LIGHT, place, tokens, theirs, key_grads
+    )
+    packed, far_plus, far_minus, plus_b, minus_a = tied(
+        packed, far_plus, far_minus, plus_b, minus_a
+    )
     far_plus, far_minus = send(far_plus, OUTER, 1), send(far_minus, OUTER, 3)
-    plus_a = add(plus_a, far_plus).astype(bf16)
-    minus_b = add(minus_b, far_minus).astype(bf16)
-    packed, plus_a, minus_b, plus_b, minus_a = tied(packed, plus_a, minus_b, plus_b, minus_a)
     plus_b, minus_a = send(plus_b, OUTER, 1), send(minus_a, OUTER, 3)
-    plus_a, minus_b = send(plus_a, OUTER, 1), send(minus_b, OUTER, 3)
     got = lax.all_to_all(packed, "fsdp", split_axis=0, concat_axis=0, tiled=True)
     seed, moments = unpack(rows_taken, got)
+    seed, plus_b, minus_a, far_plus, far_minus = tied(seed, plus_b, minus_a, far_plus, far_minus)
+    plus_a, minus_b = gradient_call(
+        joined_gradient_kernel, 2, (), LIGHT, place, tokens, theirs, grads_t, far_plus, far_minus
+    )
+    two = jnp.stack([seed, send(seed, PAIR)])
+    two, plus_a, minus_b = tied(two, plus_a, minus_b)
+    plus_a, minus_b = send(plus_a, OUTER, 1), send(minus_b, OUTER, 3)
     u = [add(stay_a[s], plus_a[s], minus_a[s]).astype(bf16) for s in range(2)]
     u += [add(stay_b[s], plus_b[s], minus_b[s]).astype(bf16) for s in range(2)]
 
-    two = jnp.stack([seed, send(seed, PAIR)])
     own = jnp.stack([two] + [send(two, INNER, s) for s in (1, 2, 3)])
 
     own, *u = tied(own, *u)

time: 197 us -> 190 us (0.964)
  blocking collectives: 0 us -> 30.5 us
  waiting for transfers between devices: 78.9 us -> 64.5 us
  starting transfers between devices: 45.3 us -> 36.7 us
  other arithmetic: 11.4 us -> 3.56 us
  Pallas kernels: 45.8 us -> 39.3 us
    all_to_all x0 -> x1, blocking collectives: none -> 30.5 us  [on_device(): lax.all_to_all(packed, 'fsdp', split_axis=0, concat_axis=0, tiled=True)]
    all_to_all x1 -> x0, waiting for transfers between devices: 9.68 us -> none  [on_device(): lax.all_to_all(packed, 'fsdp', split_axis=0, concat_axis=0, tiled=True)]
    all_to_all x1 -> x0, starting transfers between devices: 7.12 us -> none  [on_device(): lax.all_to_all(packed, 'fsdp', split_axis=0, concat_axis=0, tiled=True)]
    convert_element_type x2 -> x0, other arithmetic: 4.88 us -> none  [the longest x1 2.44 us: on_device(): plus_a = add(plus_a, far_plus).astype(bf16)]
    pallas_call x3, Pallas kernels: 17.4 us -> 12.6 us  [the longest x2 9.38 us: gradient_call(): pl.pallas_call(kernel, out_shape=(half,) * halves + others, in_specs=[SME...]
    ppermute x28, waiting for transfers between devices: 69.2 us -> 64.5 us  [send(): return lax.ppermute(array, AXES, shift_pairs(axis_of_core, shift))]
    unnamed x46 -> x36, local copies, waits for them, and re-layouts: 11.9 us -> 10.6 us
  transfers between devices with their start and end apart: 29 -> 28, of which waited for: 14 -> 11; matrix products, arithmetic and copies ran while one was open for 5% -> 3% of each run, Pallas kernels for 11% -> 11%
where the time goes in v3:
time: 190 us
  waiting for transfers between devices  64.5 us (34%)
  Pallas kernels  39.3 us (21%)
  starting transfers between devices  36.7 us (19%)
  blocking collectives  30.5 us (16%)
  local copies, waits for them, and re-layouts  14 us (7%)
  other arithmetic  3.56 us (2%)
    ppermute x28, waiting for transfers between devices, send(): return lax.ppermute(array, AXES, shift_pairs(axis_of_core, shift))  64.5 us
    ppermute x28, starting transfers between devices, send(): return lax.ppermute(array, AXES, shift_pairs(axis_of_core, shift))  36.7 us
    all_to_all x1, blocking collectives, on_device(): lax.all_to_all(packed, 'fsdp', split_axis=0, concat_axis=0, tiled=True)  30.5 us
    pallas_call x1, Pallas kernels, near_products(): pl.pallas_call(near_kernel, out_shape=(jax.ShapeDtypeStruct((TOK, C), f32...  11.7 us
    unnamed x36, local copies, waits for them, and re-layouts  10.6 us
    pallas_call x1, Pallas kernels, far_products(): pl.pallas_call(far_kernel, out_shape=(jax.ShapeDtypeStruct((TOK, C), bf16...  10 us
    pallas_call x2, Pallas kernels, gradient_call(): pl.pallas_call(kernel, out_shape=(half,) * halves + others, in_specs=[SME...  9.38 us
  transfers between devices with their start and end apart: 28, of which 11 were waited for; matrix products, arithmetic and copies ran while one was open for 3% of the time, Pallas kernels for 11%

profile of v3, /device:TPU:1, one launch (start us, length us, event | category | flops | bytes accessed | tf_op | source)
XLA Modules:
  0.0 189.9 jit_solution(4320673847583813379)
XLA Ops:
  0.8 3.4 %copy-done = bf16[256,16384]{1,0:T(8,128)(2,1)S(1)} copy-done((bf16[256,16384]{1,0:T(8,128)(2,1)S(1)}, bf16[256,16384]{1,0:T(8,128)(2,1)}, u32[]{:S(2)}) %copy-start) | copy-done | bytes 8388632
  5.1 3.2 %shard_map.101 = bf16[256,8704]{1,0:T(8,128)(2,1)} custom-call(s32[5]{0:T(128)S(1)} %stack.56.place, bf16[256,16384]{1,0:T(8,128)(2,1)S(1)} %copy-done, bf16[256,512]{1,0:T(8,128)(2,1)S(1)} %copy-done.2), custom_call_target="tpu_custom_call" | custom-call | bytes 1024 | tf_op jit(solution)/shard_map/pallas_call | solution.py:75
  11.1 1.6 copy-done.5
  13.6 3.6 %collective-permute-done.theirs = bf16[256,8704]{1,0:T(8,128)(2,1)} collective-permute-done((bf16[256,8704]{1,0:T(8,128)(2,1)}, bf16[256,8704]{1,0:T(8,128)(2,1)}, u32[]{:S(2)}, u32[]{:S(2)}) %collective-permute-start) | collective-permute-done | bytes 4456480 | tf_op jit(solution)/shard_map/ppermute | solution.py:56
  17.3 3.4 %copy-done.1 = bf16[256,16384]{1,0:T(8,128)(2,1)S(1)} copy-done((bf16[256,16384]{1,0:T(8,128)(2,1)S(1)}, bf16[256,16384]{1,0:T(8,128)(2,1)}, u32[]{:S(2)}) %copy-start.1) | copy-done | bytes 8388632
  20.7 5.8 %shard_map.103 = (bf16[2,2,512,256]{3,2,1,0:T(8,128)(2,1)S(1)}, bf16[2,2,512,256]{3,2,1,0:T(8,128)(2,1)S(1)}, bf16[2,2,512,256]{3,2,1,0:T(8,128)(2,1)S(1)}, bf16...) custom-call(s32[5]{0:T(128)S(1)} %stack.56.place, ...), custom_call_target="tpu_custom_call" | custom-call | bytes 1024 | tf_op jit(solution)/shard_map/pallas_call | solution.py:188
  29.4 2.7 %collective-permute-start.4 = (bf16[2,2,512,256]{3,2,1,0:T(8,128)(2,1)S(1)}, bf16[2,2,512,256]{3,2,1,0:T(8,128)(2,1)S(1)}, u32[]{:S(2)}, u32[]{:S(2)}) collective-permute-start(bf16[2,2,512,256]{3,2,1,0:T(8,128)(2,1)S(1)} %get-tuple-element.65), channel_id=1, source_target_pairs={{0,12},{1,49},{2,14},{3,51},{64,76},{65,113},{66,78},{67,115},{16,... | collective-permute-start | bytes 3145736 | tf_op jit(solution)/shard_map/ppermute | solution.py:56
  32.1 30.5 %all_to_all.11 = bf16[32,32,512]{2,1,0:T(8,128)(2,1)S(1)} all-to-all(bf16[32,32,512]{2,1,0:T(8,128)(2,1)S(1)} %bitcast.32), channel_id=1, replica_groups=mesh['fsdp'=32,'dp'=4] {'fsdp'}, dimensions={0} | all-to-all | bytes 2097152 | tf_op jit(solution)/shard_map/all_to_all | solution.py:408
  63.4 3.6 %shard_map.105 = (bf16[2,2,512,256]{3,2,1,0:T(8,128)(2,1)S(1)}, bf16[2,2,512,256]{3,2,1,0:T(8,128)(2,1)S(1)}) custom-call(s32[5]{0:T(128)S(1)} %stack.56.place, bf16[256,16384]{1,0:T(8,128)(2,1)S(1)} %copy-done.1, bf16[256,8704]{1,0:T(8,128)(2,1)} %collective-permute-done.theirs, bf16[512,512]{1,0:T(8,128)(2,1)S(1)} %get-tuple-element.67.grads_t, ...), custom_call_target="tpu_custom_call" | custom-call | bytes 1024 | tf_op jit(solution)/shard_map/pallas_call | solution.py:188
  67.0 3.1 %collective-permute-done.5 = bf16[512,256]{1,0:T(8,128)(2,1)S(1)} collective-permute-done((bf16[512,256]{1,0:T(8,128)(2,1)S(1)}, bf16[512,256]{1,0:T(8,128)(2,1)S(1)}, u32[]{:S(2)}, u32[]{:S(2)}) %collective-permute-start.5) | collective-permute-done | bytes 262176 | tf_op jit(solution)/shard_map/ppermute | solution.py:56
  70.6 2.3 %collective-permute-start.10 = (bf16[2,2,512,256]{3,2,1,0:T(8,128)(2,1)S(1)}, bf16[2,2,512,256]{3,2,1,0:T(8,128)(2,1)S(1)}, u32[]{:S(2)}, u32[]{:S(2)}) collective-permute-start(bf16[2,2,512,256]{3,2,1,0:T(8,128)(2,1)S(1)} %get-tuple-element.78), channel_id=1, source_target_pairs={{0,12},{1,49},{2,14},{3,51},{64,76},{65,113},{66,78},{67,115},{16,... | collective-permute-start | bytes 3145736 | tf_op jit(solution)/shard_map/ppermute | solution.py:56
  72.9 2.2 %collective-permute-start.8 = (bf16[2,512,256]{2,1,0:T(8,128)(2,1)S(1)}, bf16[2,512,256]{2,1,0:T(8,128)(2,1)S(1)}, u32[]{:S(2)}, u32[]{:S(2)}) collective-permute-start(bf16[2,512,256]{2,1,0:T(8,128)(2,1)S(1)} %pad_maximum_fusion.1), channel_id=1, source_target_pairs={{0,48},{1,13},{2,50},{3,15},{64,112},{65,77},{66,114},{67,79},{16,... | collective-permute-start | bytes 1572872 | tf_op jit(solution)/shard_map/ppermute | solution.py:56
  75.1 2.5 %collective-permute-start.7 = (bf16[2,512,256]{2,1,0:T(8,128)(2,1)S(1)}, bf16[2,512,256]{2,1,0:T(8,128)(2,1)S(1)}, u32[]{:S(2)}, u32[]{:S(2)}) collective-permute-start(bf16[2,512,256]{2,1,0:T(8,128)(2,1)S(1)} %pad_maximum_fusion.1), channel_id=1, source_target_pairs={{0,32},{1,9},{2,34},{3,11},{64,96},{65,73},{66,98},{67,75},{16,48}... | collective-permute-start | bytes 1572872 | tf_op jit(solution)/shard_map/ppermute | solution.py:56
  78.5 3.5 %collective-permute-done.8 = bf16[2,512,256]{2,1,0:T(8,128)(2,1)S(1)} collective-permute-done((bf16[2,512,256]{2,1,0:T(8,128)(2,1)S(1)}, bf16[2,512,256]{2,1,0:T(8,128)(2,1)S(1)}, u32[]{:S(2)}, u32[]{:S(2)}) %collective-permute-start.8) | collective-permute-done | bytes 524320 | tf_op jit(solution)/shard_map/ppermute | solution.py:56
  82.0 7.1 %collective-permute-done.7 = bf16[2,512,256]{2,1,0:T(8,128)(2,1)S(1)} collective-permute-done((bf16[2,512,256]{2,1,0:T(8,128)(2,1)S(1)}, bf16[2,512,256]{2,1,0:T(8,128)(2,1)S(1)}, u32[]{:S(2)}, u32[]{:S(2)}) %collective-permute-start.7) | collective-permute-done | bytes 524320 | tf_op jit(solution)/shard_map/ppermute | solution.py:56
  89.1 11.2 %collective-permute-done.6 = bf16[2,512,256]{2,1,0:T(8,128)(2,1)S(1)} collective-permute-done((bf16[2,512,256]{2,1,0:T(8,128)(2,1)S(1)}, bf16[2,512,256]{2,1,0:T(8,128)(2,1)S(1)}, u32[]{:S(2)}, u32[]{:S(2)}) %collective-permute-start.6) | collective-permute-done | bytes 524320 | tf_op jit(solution)/shard_map/ppermute | solution.py:56
  101.5 2.7 %collective-permute-start.15 = (bf16[4,2,512,256]{3,2,1,0:T(8,128)(2,1)S(1)}, bf16[4,2,512,256]{3,2,1,0:T(8,128)(2,1)S(1)}, u32[]{:S(2)}, u32[]{:S(2)}) collective-permute-start(bf16[4,2,512,256]{3,2,1,0:T(8,128)(2,1)S(1)} %pad_maximum_fusion.refs_0_), channel_id=1, source_target_pairs={{0,12},{1,49},{2,14},{3,51},{64,76},{65,113},{66,78},{67,115},{16,... | collective-permute-start | bytes 6291464 | tf_op jit(solution)/shard_map/ppermute | solution.py:56
  104.5 1.8 collective-permute-start.12
  106.3 1.8 collective-permute-start.11
  108.1 10.6 %collective-permute-done.13 = bf16[2,512,256]{2,1,0:T(8,128)(2,1)S(1)} collective-permute-done((bf16[2,512,256]{2,1,0:T(8,128)(2,1)S(1)}, bf16[2,512,256]{2,1,0:T(8,128)(2,1)S(1)}, u32[]{:S(2)}, u32[]{:S(2)}) %collective-permute-start.13) | collective-permute-done | bytes 524320 | tf_op jit(solution)/shard_map/ppermute | solution.py:56
  118.8 2.7 %collective-permute-start.19 = (bf16[4,2,512,256]{3,2,1,0:T(8,128)(2,1)S(1)}, bf16[4,2,512,256]{3,2,1,0:T(8,128)(2,1)S(1)}, u32[]{:S(2)}, u32[]{:S(2)}) collective-permute-start(bf16[4,2,512,256]{3,2,1,0:T(8,128)(2,1)S(1)} %pad_maximum_fusion.refs_0_), channel_id=1, source_target_pairs={{0,1},{1,0},{2,3},{3,2},{64,65},{65,64},{66,67},{67,66},{16,17},{1... | collective-permute-start | bytes 6291464 | tf_op jit(solution)/shard_map/ppermute | solution.py:56
  121.5 10.4 %collective-permute-done.11 = bf16[2,512,256]{2,1,0:T(8,128)(2,1)S(1)} collective-permute-done((bf16[2,512,256]{2,1,0:T(8,128)(2,1)S(1)}, bf16[2,512,256]{2,1,0:T(8,128)(2,1)S(1)}, u32[]{:S(2)}, u32[]{:S(2)}) %collective-permute-start.11) | collective-permute-done | bytes 524320 | tf_op jit(solution)/shard_map/ppermute | solution.py:56
  132.0 7.0 %collective-permute-done.14.refs_1_ = bf16[4,2,512,256]{3,2,1,0:T(8,128)(2,1)S(1)} collective-permute-done((bf16[4,2,512,256]{3,2,1,0:T(8,128)(2,1)S(1)}, bf16[4,2,512,256]{3,2,1,0:T(8,128)(2,1)S(1)}, u32[]{:S(2)}, u32[]{:S(2)}) %collective-permute-start.14) | collective-permute-done | bytes 2097184 | tf_op jit(solution)/shard_map/ppermute | solution.py:56
  139.1 2.9 %collective-permute-start.20 = (bf16[4,2,512,256]{3,2,1,0:T(8,128)(2,1)S(1)}, bf16[4,2,512,256]{3,2,1,0:T(8,128)(2,1)S(1)}, u32[]{:S(2)}, u32[]{:S(2)}) collective-permute-start(bf16[4,2,512,256]{3,2,1,0:T(8,128)(2,1)S(1)} %collective-permute-done.14.refs_1_), channel_id=1, source_target_pairs={{0,1},{1,0},{2,3},{3,2},{64,65},{65,64},{66,67},{67,66},{16,17},{1... | collective-permute-start | bytes 6291464 | tf_op jit(solution)/shard_map/ppermute | solution.py:56
  144.1 5.4 %collective-permute-done.18 = bf16[512,256]{1,0:T(8,128)(2,1)S(1)} collective-permute-done((bf16[512,256]{1,0:T(8,128)(2,1)S(1)}, bf16[512,256]{1,0:T(8,128)(2,1)S(1)}, u32[]{:S(2)}, u32[]{:S(2)}) %collective-permute-start.18) | collective-permute-done | bytes 262176 | tf_op jit(solution)/shard_map/ppermute | solution.py:56
  150.5 3.4 %collective-permute-start.22 = (bf16[512,256]{1,0:T(8,128)(2,1)S(1)}, bf16[512,256]{1,0:T(8,128)(2,1)S(1)}, u32[]{:S(2)}, u32[]{:S(2)}) collective-permute-start(bf16[512,256]{1,0:T(8,128)(2,1)S(1)} %fusion.4), channel_id=1, source_target_pairs={{0,2},{1,3},{2,0},{3,1},{64,66},{65,67},{66,64},{67,65},{16,18},{1... | collective-permute-start | bytes 786440 | tf_op jit(solution)/shard_map/ppermute | solution.py:56
  153.9 2.5 %collective-permute-start.25 = (bf16[512,256]{1,0:T(8,128)(2,1)S(1)}, bf16[512,256]{1,0:T(8,128)(2,1)}, u32[]{:S(2)}, u32[]{:S(2)}) collective-permute-start(bf16[512,256]{1,0:T(8,128)(2,1)S(1)} %get-tuple-element.99), channel_id=1, source_target_pairs={{0,2},{1,3},{2,0},{3,1},{64,66},{65,67},{66,64},{67,65},{16,18},{1... | collective-permute-start | bytes 786440 | tf_op jit(solution)/shard_map/ppermute | solution.py:56
  156.4 11.7 %shard_map.106 = (f32[256,512]{1,0:T(8,128)}, bf16[256,16384]{1,0:T(8,128)(2,1)}) custom-call(s32[5]{0:T(128)} %copy-done.7, bf16[256,16384]{1,0:T(8,128)(2,1)} %tokens.9, bf16[256,512]{1,0:T(8,128)(2,1)} %key_grads.7, bf16[4,2,512,256]{3,2,1,0:T(8,128)(2,1)} %copy-done.9, bf16[4,2,512,256]{3,2,1,0:T(8,128)(2,1)} %copy-done.10, ...), custom_call_target="tpu_custom_call" | custom-call | bytes 1024 | tf_op jit(solution)/shard_map/pallas_call | solution.py:285
  168.2 1.6 collective-permute-start.23
  172.5 1.8 collective-permute-done.27.refs_2_
  175.1 3.3 %shard_map.108 = (bf16[512,512]{1,0:T(8,128)(2,1)}, f32[512,512]{1,0:T(8,128)}, f32[512,512]{1,0:T(8,128)}) custom-call(s32[5]{0:T(128)S(1)} %copy-done.8, f32[512,256]{1,0:T(8,128)S(1)} %convert_add_fusion.grads, bf16[512,256]{1,0:T(8,128)(2,1)S(1)} %get-tuple-element.66.weights, bf16[512,512]{1,0:T(8,128)(2,1)S(1)} %pad_maximum_fusion.2.moments, ...), custom_call_target="tpu_custom_call" | custom-call | bytes 1024 | tf_op jit(solution)/shard_map/pallas_call | solution.py:372
  179.7 10.0 %shard_map.107 = (bf16[256,512]{1,0:T(8,128)(2,1)}, bf16[256,16384]{1,0:T(8,128)(2,1)}) custom-call(s32[5]{0:T(128)} %copy-done.7, bf16[256,16384]{1,0:T(8,128)(2,1)} %tokens.9, bf16[256,512]{1,0:T(8,128)(2,1)} %key_grads.7, f32[256,512]{1,0:T(8,128)} %get-tuple-element.92.start, ...), custom_call_target="tpu_custom_call", output_to_operand_aliasing={{1}: (4, {})} | custom-call | bytes 1024 | tf_op jit(solution)/shard_map/pallas_call | solution.py:300
  (91 shorter events, 19.4 us)
Async XLA Ops:
  5.1 58.3 %copy-start.7 = (s32[5]{0:T(128)}, s32[5]{0:T(128)S(1)}, u32[]{:S(2)}) copy-start(s32[5]{0:T(128)S(1)} %stack.56.place) | copy-start | bytes 64
  5.1 5.9 %copy-start.6 = (bf16[1024,512]{1,0:T(8,128)(2,1)S(1)}, bf16[1024,512]{1,0:T(8,128)(2,1)}, u32[]{:S(2)}) copy-start(bf16[1024,512]{1,0:T(8,128)(2,1)} %param.13) | copy-start | bytes 3145732
  8.3 8.9 %collective-permute-start = (bf16[256,8704]{1,0:T(8,128)(2,1)}, bf16[256,8704]{1,0:T(8,128)(2,1)}, u32[]{:S(2)}, u32[]{:S(2)}) collective-permute-start(bf16[256,8704]{1,0:T(8,128)(2,1)} %shard_map.101), channel_id=1, source_target_pairs={{0,1},{1,0},{2,3},{3,2},{64,65},{65,64},{66,67},{67,66},{16,17},{1... | collective-permute-start | bytes 13369352 | tf_op jit(solution)/shard_map/ppermute | solution.py:56
  26.5 36.8 %collective-permute-start.1 = (bf16[2,2,512,256]{3,2,1,0:T(8,128)(2,1)S(1)}, bf16[2,2,512,256]{3,2,1,0:T(8,128)(2,1)S(1)}, u32[]{:S(2)}, u32[]{:S(2)}) collective-permute-start(bf16[2,2,512,256]{3,2,1,0:T(8,128)(2,1)S(1)} %get-tuple-element.62), channel_id=1, source_target_pairs={{0,4},{1,17},{2,6},{3,19},{64,68},{65,81},{66,70},{67,83},{16,20},... | collective-permute-start | bytes 3145736 | tf_op jit(solution)/shard_map/ppermute | solution.py:56
  27.9 35.4 %collective-permute-start.2 = (bf16[2,2,512,256]{3,2,1,0:T(8,128)(2,1)S(1)}, bf16[2,2,512,256]{3,2,1,0:T(8,128)(2,1)S(1)}, u32[]{:S(2)}, u32[]{:S(2)}) collective-permute-start(bf16[2,2,512,256]{3,2,1,0:T(8,128)(2,1)S(1)} %get-tuple-element.63), channel_id=1, source_target_pairs={{0,12},{1,49},{2,14},{3,51},{64,76},{65,113},{66,78},{67,115},{16,... | collective-permute-start | bytes 3145736 | tf_op jit(solution)/shard_map/ppermute | solution.py:56
  29.4 33.9 %collective-permute-start.3 = (bf16[2,2,512,256]{3,2,1,0:T(8,128)(2,1)S(1)}, bf16[2,2,512,256]{3,2,1,0:T(8,128)(2,1)S(1)}, u32[]{:S(2)}, u32[]{:S(2)}) collective-permute-start(bf16[2,2,512,256]{3,2,1,0:T(8,128)(2,1)S(1)} %get-tuple-element.64), channel_id=1, source_target_pairs={{0,4},{1,17},{2,6},{3,19},{64,68},{65,81},{66,70},{67,83},{16,20},... | collective-permute-start | bytes 3145736 | tf_op jit(solution)/shard_map/ppermute | solution.py:56
  29.4 33.9 %collective-permute-start.4 = (bf16[2,2,512,256]{3,2,1,0:T(8,128)(2,1)S(1)}, bf16[2,2,512,256]{3,2,1,0:T(8,128)(2,1)S(1)}, u32[]{:S(2)}, u32[]{:S(2)}) collective-permute-start(bf16[2,2,512,256]{3,2,1,0:T(8,128)(2,1)S(1)} %get-tuple-element.65), channel_id=1, source_target_pairs={{0,12},{1,49},{2,14},{3,51},{64,76},{65,113},{66,78},{67,115},{16,... | collective-permute-start | bytes 3145736 | tf_op jit(solution)/shard_map/ppermute | solution.py:56
  63.3 6.8 %collective-permute-start.5 = (bf16[512,256]{1,0:T(8,128)(2,1)S(1)}, bf16[512,256]{1,0:T(8,128)(2,1)S(1)}, u32[]{:S(2)}, u32[]{:S(2)}) collective-permute-start(bf16[512,256]{1,0:T(8,128)(2,1)S(1)} %get-tuple-element.66.weights), channel_id=1, source_target_pairs={{0,64},{1,65},{2,66},{3,67},{64,0},{65,1},{66,2},{67,3},{16,80},{1... | collective-permute-start | bytes 786440 | tf_op jit(solution)/shard_map/ppermute | solution.py:56
  70.2 30.3 %collective-permute-start.9 = (bf16[2,2,512,256]{3,2,1,0:T(8,128)(2,1)S(1)}, bf16[2,2,512,256]{3,2,1,0:T(8,128)(2,1)S(1)}, u32[]{:S(2)}, u32[]{:S(2)}) collective-permute-start(bf16[2,2,512,256]{3,2,1,0:T(8,128)(2,1)S(1)} %get-tuple-element.74), channel_id=1, source_target_pairs={{0,4},{1,17},{2,6},{3,19},{64,68},{65,81},{66,70},{67,83},{16,20},... | collective-permute-start | bytes 3145736 | tf_op jit(solution)/shard_map/ppermute | solution.py:56
  70.6 30.4 %collective-permute-start.10 = (bf16[2,2,512,256]{3,2,1,0:T(8,128)(2,1)S(1)}, bf16[2,2,512,256]{3,2,1,0:T(8,128)(2,1)S(1)}, u32[]{:S(2)}, u32[]{:S(2)}) collective-permute-start(bf16[2,2,512,256]{3,2,1,0:T(8,128)(2,1)S(1)} %get-tuple-element.78), channel_id=1, source_target_pairs={{0,12},{1,49},{2,14},{3,51},{64,76},{65,113},{66,78},{67,115},{16,... | collective-permute-start | bytes 3145736 | tf_op jit(solution)/shard_map/ppermute | solution.py:56
  72.9 9.0 %collective-permute-start.8 = (bf16[2,512,256]{2,1,0:T(8,128)(2,1)S(1)}, bf16[2,512,256]{2,1,0:T(8,128)(2,1)S(1)}, u32[]{:S(2)}, u32[]{:S(2)}) collective-permute-start(bf16[2,512,256]{2,1,0:T(8,128)(2,1)S(1)} %pad_maximum_fusion.1), channel_id=1, source_target_pairs={{0,48},{1,13},{2,50},{3,15},{64,112},{65,77},{66,114},{67,79},{16,... | collective-permute-start | bytes 1572872 | tf_op jit(solution)/shard_map/ppermute | solution.py:56
  75.1 13.9 %collective-permute-start.7 = (bf16[2,512,256]{2,1,0:T(8,128)(2,1)S(1)}, bf16[2,512,256]{2,1,0:T(8,128)(2,1)S(1)}, u32[]{:S(2)}, u32[]{:S(2)}) collective-permute-start(bf16[2,512,256]{2,1,0:T(8,128)(2,1)S(1)} %pad_maximum_fusion.1), channel_id=1, source_target_pairs={{0,32},{1,9},{2,34},{3,11},{64,96},{65,73},{66,98},{67,75},{16,48}... | collective-permute-start | bytes 1572872 | tf_op jit(solution)/shard_map/ppermute | solution.py:56
  77.6 22.6 %collective-permute-start.6 = (bf16[2,512,256]{2,1,0:T(8,128)(2,1)S(1)}, bf16[2,512,256]{2,1,0:T(8,128)(2,1)S(1)}, u32[]{:S(2)}, u32[]{:S(2)}) collective-permute-start(bf16[2,512,256]{2,1,0:T(8,128)(2,1)S(1)} %pad_maximum_fusion.1), channel_id=1, source_target_pairs={{0,16},{1,5},{2,18},{3,7},{64,80},{65,69},{66,82},{67,71},{16,32},... | collective-permute-start | bytes 1572872 | tf_op jit(solution)/shard_map/ppermute | solution.py:56
  100.5 18.3 %copy-start.9 = (bf16[4,2,512,256]{3,2,1,0:T(8,128)(2,1)}, bf16[4,2,512,256]{3,2,1,0:T(8,128)(2,1)S(1)}, u32[]{:S(2)}) copy-start(bf16[4,2,512,256]{3,2,1,0:T(8,128)(2,1)S(1)} %pad_maximum_fusion.refs_0_) | copy-start | bytes 6291460
  101.4 37.7 %collective-permute-start.14 = (bf16[4,2,512,256]{3,2,1,0:T(8,128)(2,1)S(1)}, bf16[4,2,512,256]{3,2,1,0:T(8,128)(2,1)S(1)}, u32[]{:S(2)}, u32[]{:S(2)}) collective-permute-start(bf16[4,2,512,256]{3,2,1,0:T(8,128)(2,1)S(1)} %pad_maximum_fusion.refs_0_), channel_id=1, source_target_pairs={{0,4},{1,17},{2,6},{3,19},{64,68},{65,81},{66,70},{67,83},{16,20},... | collective-permute-start | bytes 6291464 | tf_op jit(solution)/shard_map/ppermute | solution.py:56
  101.5 37.6 %collective-permute-start.15 = (bf16[4,2,512,256]{3,2,1,0:T(8,128)(2,1)S(1)}, bf16[4,2,512,256]{3,2,1,0:T(8,128)(2,1)S(1)}, u32[]{:S(2)}, u32[]{:S(2)}) collective-permute-start(bf16[4,2,512,256]{3,2,1,0:T(8,128)(2,1)S(1)} %pad_maximum_fusion.refs_0_), channel_id=1, source_target_pairs={{0,12},{1,49},{2,14},{3,51},{64,76},{65,113},{66,78},{67,115},{16,... | collective-permute-start | bytes 6291464 | tf_op jit(solution)/shard_map/ppermute | solution.py:56
  104.1 14.6 %collective-permute-start.13 = (bf16[2,512,256]{2,1,0:T(8,128)(2,1)S(1)}, bf16[2,512,256]{2,1,0:T(8,128)(2,1)S(1)}, u32[]{:S(2)}, u32[]{:S(2)}) collective-permute-start(bf16[2,512,256]{2,1,0:T(8,128)(2,1)S(1)} %get-tuple-element.82), channel_id=1, source_target_pairs={{0,48},{1,13},{2,50},{3,15},{64,112},{65,77},{66,114},{67,79},{16,... | collective-permute-start | bytes 1572872 | tf_op jit(solution)/shard_map/ppermute | solution.py:56
  104.5 17.0 %collective-permute-start.12 = (bf16[2,512,256]{2,1,0:T(8,128)(2,1)S(1)}, bf16[2,512,256]{2,1,0:T(8,128)(2,1)S(1)}, u32[]{:S(2)}, u32[]{:S(2)}) collective-permute-start(bf16[2,512,256]{2,1,0:T(8,128)(2,1)S(1)} %get-tuple-element.81), channel_id=1, source_target_pairs={{0,16},{1,5},{2,18},{3,7},{64,80},{65,69},{66,82},{67,71},{16,32},... | collective-permute-start | bytes 1572872 | tf_op jit(solution)/shard_map/ppermute | solution.py:56
  106.3 25.6 %collective-permute-start.11 = (bf16[2,512,256]{2,1,0:T(8,128)(2,1)S(1)}, bf16[2,512,256]{2,1,0:T(8,128)(2,1)S(1)}, u32[]{:S(2)}, u32[]{:S(2)}) collective-permute-start(bf16[2,512,256]{2,1,0:T(8,128)(2,1)S(1)} %get-tuple-element.80), channel_id=1, source_target_pairs={{0,32},{1,9},{2,34},{3,11},{64,96},{65,73},{66,98},{67,75},{16,48}... | collective-permute-start | bytes 1572872 | tf_op jit(solution)/shard_map/ppermute | solution.py:56
  118.8 31.7 %collective-permute-start.19 = (bf16[4,2,512,256]{3,2,1,0:T(8,128)(2,1)S(1)}, bf16[4,2,512,256]{3,2,1,0:T(8,128)(2,1)S(1)}, u32[]{:S(2)}, u32[]{:S(2)}) collective-permute-start(bf16[4,2,512,256]{3,2,1,0:T(8,128)(2,1)S(1)} %pad_maximum_fusion.refs_0_), channel_id=1, source_target_pairs={{0,1},{1,0},{2,3},{3,2},{64,65},{65,64},{66,67},{67,66},{16,17},{1... | collective-permute-start | bytes 6291464 | tf_op jit(solution)/shard_map/ppermute | solution.py:56
  139.1 11.4 %collective-permute-start.20 = (bf16[4,2,512,256]{3,2,1,0:T(8,128)(2,1)S(1)}, bf16[4,2,512,256]{3,2,1,0:T(8,128)(2,1)S(1)}, u32[]{:S(2)}, u32[]{:S(2)}) collective-permute-start(bf16[4,2,512,256]{3,2,1,0:T(8,128)(2,1)S(1)} %collective-permute-done.14.refs_1_), channel_id=1, source_target_pairs={{0,1},{1,0},{2,3},{3,2},{64,65},{65,64},{66,67},{67,66},{16,17},{1... | collective-permute-start | bytes 6291464 | tf_op jit(solution)/shard_map/ppermute | solution.py:56
  141.9 8.5 %collective-permute-start.21 = (bf16[4,2,512,256]{3,2,1,0:T(8,128)(2,1)S(1)}, bf16[4,2,512,256]{3,2,1,0:T(8,128)(2,1)S(1)}, u32[]{:S(2)}, u32[]{:S(2)}) collective-permute-start(bf16[4,2,512,256]{3,2,1,0:T(8,128)(2,1)S(1)} %collective-permute-done.15.refs_2_), channel_id=1, source_target_pairs={{0,1},{1,0},{2,3},{3,2},{64,65},{65,64},{66,67},{67,66},{16,17},{1... | collective-permute-start | bytes 6291464 | tf_op jit(solution)/shard_map/ppermute | solution.py:56
  142.0 7.5 %collective-permute-start.18 = (bf16[512,256]{1,0:T(8,128)(2,1)S(1)}, bf16[512,256]{1,0:T(8,128)(2,1)S(1)}, u32[]{:S(2)}, u32[]{:S(2)}) collective-permute-start(bf16[512,256]{1,0:T(8,128)(2,1)S(1)} %fusion.5), channel_id=1, source_target_pairs={{0,64},{1,65},{2,66},{3,67},{64,0},{65,1},{66,2},{67,3},{16,80},{1... | collective-permute-start | bytes 786440 | tf_op jit(solution)/shard_map/ppermute | solution.py:56
  144.1 24.1 %collective-permute-start.16 = (bf16[2,2,512,256]{3,2,1,0:T(8,128)(2,1)}, bf16[2,2,512,256]{3,2,1,0:T(8,128)(2,1)}, u32[]{:S(2)}, u32[]{:S(2)}) collective-permute-start(bf16[2,2,512,256]{3,2,1,0:T(8,128)(2,1)} %slice.97), channel_id=1, source_target_pairs={{0,4},{1,17},{2,6},{3,19},{64,68},{65,81},{66,70},{67,83},{16,20},... | collective-permute-start | bytes 3145736 | tf_op jit(solution)/shard_map/ppermute | solution.py:56
  149.5 18.7 %collective-permute-start.17 = (bf16[2,2,512,256]{3,2,1,0:T(8,128)(2,1)}, bf16[2,2,512,256]{3,2,1,0:T(8,128)(2,1)}, u32[]{:S(2)}, u32[]{:S(2)}) collective-permute-start(bf16[2,2,512,256]{3,2,1,0:T(8,128)(2,1)} %slice.98), channel_id=1, source_target_pairs={{0,12},{1,49},{2,14},{3,51},{64,76},{65,113},{66,78},{67,115},{16,... | collective-permute-start | bytes 3145736 | tf_op jit(solution)/shard_map/ppermute | solution.py:56
  150.5 17.7 %collective-permute-start.22 = (bf16[512,256]{1,0:T(8,128)(2,1)S(1)}, bf16[512,256]{1,0:T(8,128)(2,1)S(1)}, u32[]{:S(2)}, u32[]{:S(2)}) collective-permute-start(bf16[512,256]{1,0:T(8,128)(2,1)S(1)} %fusion.4), channel_id=1, source_target_pairs={{0,2},{1,3},{2,0},{3,1},{64,66},{65,67},{66,64},{67,65},{16,18},{1... | collective-permute-start | bytes 786440 | tf_op jit(solution)/shard_map/ppermute | solution.py:56
  153.9 16.0 %collective-permute-start.25 = (bf16[512,256]{1,0:T(8,128)(2,1)S(1)}, bf16[512,256]{1,0:T(8,128)(2,1)}, u32[]{:S(2)}, u32[]{:S(2)}) collective-permute-start(bf16[512,256]{1,0:T(8,128)(2,1)S(1)} %get-tuple-element.99), channel_id=1, source_target_pairs={{0,2},{1,3},{2,0},{3,1},{64,66},{65,67},{66,64},{67,65},{16,18},{1... | collective-permute-start | bytes 786440 | tf_op jit(solution)/shard_map/ppermute | solution.py:56
  168.1 6.9 %copy-start.8 = (s32[5]{0:T(128)S(1)}, s32[5]{0:T(128)}, u32[]{:S(2)}) copy-start(s32[5]{0:T(128)} %copy-done.7) | copy-start | bytes 64
  168.2 10.1 %collective-permute-start.23 = (bf16[2,2,512,256]{3,2,1,0:T(8,128)(2,1)}, bf16[2,2,512,256]{3,2,1,0:T(8,128)(2,1)S(1)}, u32[]{:S(2)}, u32[]{:S(2)}) collective-permute-start(bf16[2,2,512,256]{3,2,1,0:T(8,128)(2,1)} %collective-permute-done.16.refs_3_), channel_id=1, source_target_pairs={{0,1},{1,0},{2,3},{3,2},{64,65},{65,64},{66,67},{67,66},{16,17},{1... | collective-permute-start | bytes 3145736 | tf_op jit(solution)/shard_map/ppermute | solution.py:56
  169.8 8.6 %collective-permute-start.24 = (bf16[2,2,512,256]{3,2,1,0:T(8,128)(2,1)}, bf16[2,2,512,256]{3,2,1,0:T(8,128)(2,1)S(1)}, u32[]{:S(2)}, u32[]{:S(2)}) collective-permute-start(bf16[2,2,512,256]{3,2,1,0:T(8,128)(2,1)} %collective-permute-done.17.refs_4_), channel_id=1, source_target_pairs={{0,1},{1,0},{2,3},{3,2},{64,65},{65,64},{66,67},{67,66},{16,17},{1... | collective-permute-start | bytes 3145736 | tf_op jit(solution)/shard_map/ppermute | solution.py:56
  171.0 3.4 %collective-permute-start.27 = (bf16[512,512]{1,0:T(8,128)(2,1)S(1)}, bf16[512,512]{1,0:T(8,128)(2,1)S(1)}, u32[]{:S(2)}, u32[]{:S(2)}) collective-permute-start(bf16[512,512]{1,0:T(8,128)(2,1)S(1)} %pad_maximum_fusion.2.moments), channel_id=1, source_target_pairs={{0,1},{1,0},{2,3},{3,2},{64,65},{65,64},{66,67},{67,66},{16,17},{1... | collective-permute-start | bytes 1572872 | tf_op jit(solution)/shard_map/ppermute | solution.py:56
  171.5 3.6 %collective-permute-start.26 = (f32[512,256]{1,0:T(8,128)S(1)}, f32[512,256]{1,0:T(8,128)S(1)}, u32[]{:S(2)}, u32[]{:S(2)}) collective-permute-start(f32[512,256]{1,0:T(8,128)S(1)} %convert_add_fusion.grads), channel_id=1, source_target_pairs={{0,1},{1,0},{2,3},{3,2},{64,65},{65,64},{66,67},{67,66},{16,17},{1... | collective-permute-start | bytes 1572872 | tf_op jit(solution)/shard_map/ppermute | solution.py:56
  (14 other events, 47.1 us)
